TPU v7x, 32 devices: a whole 2x2x4 slice. The times are simulated.
32 devices in a mesh: node: 16 (over z, x, core), local: 2 (over y).
Axes of the slice: x: 2, y: 2, z: 4, core: 2. Of those that a mesh axis runs over, the one named last changes fastest.
Arguments:
- hidden_in: bfloat16 [6144, 14848], P(('node', 'local')), may hold values from -6 to 6
- grad_heads: bfloat16 [6144, 192], P(('node', 'local')), may hold values from -6 to 6
- w_qkv: bfloat16 [14848, 320], P(('local', 'node'))
- ln_gain: bfloat16 [14848], P(('local', 'node')), may hold values from 0.099609375 to 1.8984375
- ln_bias: bfloat16 [14848], P(('local', 'node')), may hold values from -3 to 3
- seq_lengths: int32 [16], P('node'), may hold values from 96 to 384, as said below
- sample_index: int32 [16], P('node'), may hold values from 0 to 8191
- priority: float32 [8192], replicated, may hold values from 0.25 to 4
Outputs:
- grad_input: bfloat16 [6144, 14848], P(('node', 'local'))
- grad_qkv: float32 [14848, 320], P(('local', 'node'))
- grad_gain: float32 [14848], P(('local', 'node'))
- grad_bias: float32 [14848], P(('local', 'node'))
Inputs may be any that keep to these rules, and one draw needn't show every extreme that they name: `seq_lengths`: exactly 384 for at least one sequence in every draw.
All inputs are finite; a program needn't handle non-finite values.
Results may differ from a plain program's by a relative error of at most 0.02.
The roundings to bfloat16 on the way count: a program that leaves them out, or rounds other values in their place, can miss the bound.
Values may be sent and summed in bfloat16 or wider, within the bound.
A program may use at most 128 MiB of HBM per device.

v0:
```python
import jax
import jax.numpy as jnp
from jax import lax
from jax.sharding import PartitionSpec as P

HD = 64
QH = 3


epsilon = 1e-05


def layer_stats(hidden):
    values = hidden.astype(jnp.float32)
    centre = jnp.mean(values, axis=-1, keepdims=True)
    shifted = values - centre
    variance = jnp.mean(shifted * shifted, axis=-1, keepdims=True)
    inverse = lax.rsqrt(variance + epsilon)
    return (shifted * inverse, inverse)


def rope_tables(positions, head_size):
    half_size = head_size // 2
    steps = 2.0 * jnp.arange(half_size, dtype=jnp.float32) / head_size
    freqs = jnp.exp(-jnp.log(10000.0) * steps)
    angles = positions.astype(jnp.float32)[:, None] * freqs[None, :]
    cosine = jnp.concatenate([jnp.cos(angles), jnp.cos(angles)], axis=1)
    sine_table = jnp.concatenate([jnp.sin(angles), jnp.sin(angles)], axis=1)
    return (cosine, sine_table)


def rotate(values, cosine, sine_table):
    half_size = values.shape[-1] // 2
    turned = jnp.concatenate([-values[..., half_size:], values[..., :half_size]], axis=-1)
    return values * cosine[:, None, :] + turned * sine_table[:, None, :]


def unrotate(values, cosine, sine_table):
    half_size = values.shape[-1] // 2
    turned = jnp.concatenate([values[..., half_size:], -values[..., :half_size]], axis=-1)
    return values * cosine[:, None, :] + turned * sine_table[:, None, :]


def on_device(hidden_in, grad_heads, w_qkv, ln_gain, ln_bias, seq_lengths, sample_index, priority):
    tok_rows, model_width = hidden_in.shape
    query_cols = QH * HD
    w_second, gain_second, bias_second = (
        lax.all_gather(w_qkv, "node", axis=0, tiled=True),
        lax.all_gather(ln_gain, "node", axis=0, tiled=True),
        lax.all_gather(ln_bias, "node", axis=0, tiled=True),
    )
    normalized, inverse = layer_stats(hidden_in)
    w_piece = lax.all_gather(w_second, "local", axis=0, tiled=True)
    gain_piece = lax.all_gather(gain_second, "local", axis=0, tiled=True)
    bias_piece = lax.all_gather(bias_second, "local", axis=0, tiled=True)
    normed_piece = (
        normalized * gain_piece.astype(jnp.float32) + bias_piece.astype(jnp.float32)
    ).astype(jnp.bfloat16)
    proj_total = jnp.dot(normed_piece, w_piece, preferred_element_type=jnp.float32)
    positions = lax.axis_index("local") * tok_rows + jnp.arange(tok_rows, dtype=jnp.int32)
    cosine, sine_table = rope_tables(positions, HD)
    query = rotate(proj_total[:, :query_cols].reshape(tok_rows, QH, HD), cosine, sine_table).astype(
        jnp.bfloat16
    )
    keys_own = rotate(proj_total[:, query_cols : query_cols + HD][:, None, :], cosine, sine_table)[
        :, 0, :
    ]
    pair_own = jnp.concatenate([keys_own, proj_total[:, query_cols + HD :]], axis=1).astype(
        jnp.bfloat16
    )
    pair_all = lax.all_gather(pair_own, "local", axis=0, tiled=True)
    seq_rows = pair_all.shape[0]
    keys_all = pair_all[:, :HD]
    values_all = pair_all[:, HD:]
    length = seq_lengths[0]
    weight = jnp.sum(jnp.where(jnp.arange(priority.shape[0]) == sample_index[0], priority, 0.0))
    scale = HD ** (-0.5)
    scores = jnp.einsum("qhd,kd->hqk", query, keys_all, preferred_element_type=jnp.float32) * scale
    key_positions = jnp.arange(seq_rows, dtype=jnp.int32)
    allowed = (key_positions[None, :] <= positions[:, None]) & (key_positions[None, :] < length)
    scores = jnp.where(allowed[None], scores, -1e30)
    row_max = jnp.max(scores, axis=-1, keepdims=True)
    exponent = jnp.exp(scores - row_max)
    attention = exponent / jnp.sum(exponent, axis=-1, keepdims=True)
    attention_b = attention.astype(jnp.bfloat16)
    head_out = jnp.einsum(
        "hqk,kd->qhd", attention_b, values_all, preferred_element_type=jnp.float32
    )
    live_rows = (positions < length).astype(jnp.float32)
    cotangent = (
        grad_heads.reshape(tok_rows, QH, HD).astype(jnp.float32) * weight * live_rows[:, None, None]
    ).astype(jnp.bfloat16)
    d_attention = jnp.einsum(
        "qhd,kd->hqk", cotangent, values_all, preferred_element_type=jnp.float32
    )
    row_delta = jnp.sum(cotangent.astype(jnp.float32) * head_out, axis=-1)
    d_scores = (attention * (d_attention - row_delta.T[:, :, None]) * scale).astype(jnp.bfloat16)
    d_query = jnp.einsum("hqk,kd->qhd", d_scores, keys_all, preferred_element_type=jnp.float32)
    d_key_term = jnp.einsum("hqk,qhd->kd", d_scores, query, preferred_element_type=jnp.float32)
    d_value_term = jnp.einsum(
        "hqk,qhd->kd", attention_b, cotangent, preferred_element_type=jnp.float32
    )
    d_pair = lax.psum_scatter(
        jnp.concatenate([d_key_term, d_value_term], axis=1),
        "local",
        scatter_dimension=0,
        tiled=True,
    )
    d_query_pre = unrotate(d_query, cosine, sine_table).reshape(tok_rows, query_cols)
    d_key_pre = unrotate(d_pair[:, None, :HD], cosine, sine_table)[:, 0, :]
    d_projected = jnp.concatenate([d_query_pre, d_key_pre, d_pair[:, HD:]], axis=1).astype(
        jnp.bfloat16
    )
    contract = (((1,), (1,)), ((), ()))
    d_normed = lax.dot_general(
        d_projected,
        lax.all_gather(w_second, "local", axis=0, tiled=True),
        contract,
        preferred_element_type=jnp.float32,
    )
    grad_hat = d_normed * gain_piece.astype(jnp.float32)
    grad_input = inverse * (
        grad_hat
        - jnp.mean(grad_hat, axis=-1, keepdims=True)
        - normalized * jnp.mean(grad_hat * normalized, axis=-1, keepdims=True)
    )
    term_weight = lax.dot_general(
        normed_piece, d_projected, (((0,), (0,)), ((), ())), preferred_element_type=jnp.float32
    )
    term_gain = jnp.sum(d_normed * normalized, axis=0)
    term_bias = jnp.sum(d_normed, axis=0)
    part_weight, part_gain, part_bias = (
        lax.psum_scatter(
            term_weight.astype(jnp.bfloat16), "local", scatter_dimension=0, tiled=True
        ).astype(jnp.float32),
        lax.psum_scatter(
            term_gain.astype(jnp.bfloat16), "local", scatter_dimension=0, tiled=True
        ).astype(jnp.float32),
        lax.psum_scatter(
            term_bias.astype(jnp.bfloat16), "local", scatter_dimension=0, tiled=True
        ).astype(jnp.float32),
    )
    grad_weight, grad_gain, grad_bias = (
        lax.psum_scatter(part_weight, "node", scatter_dimension=0, tiled=True),
        lax.psum_scatter(part_gain, "node", scatter_dimension=0, tiled=True),
        lax.psum_scatter(part_bias, "node", scatter_dimension=0, tiled=True),
    )
    return (grad_input.astype(jnp.bfloat16), grad_weight, grad_gain, grad_bias)


def solution(mesh):
    return jax.shard_map(
        on_device,
        mesh=mesh,
        in_specs=(
            P(("node", "local"), None),
            P(("node", "local"), None),
            P(("local", "node"), None),
            P(("local", "node")),
            P(("local", "node")),
            P("node"),
            P("node"),
            P(),
        ),
        out_specs=(
            P(("node", "local"), None),
            P(("local", "node"), None),
            P(("local", "node")),
            P(("local", "node")),
        ),
        check_vma=False,
    )
```

profile of v0, /device:TPU:0, one launch (start us, length us, event | category | flops | bytes accessed | tf_op | source)
XLA Modules:
  0.0 504.7 jit_solution(9237675342576251494)
XLA Ops:
  7.2 0.7 all-gather.8.cloned.1.call-update
  8.0 61.0 %all-gather.8.cloned.1.call-done = bf16[16,464,320]{1,2,0:T(8,128)(2,1)} async-done(((bf16[1,464,320]{1,2,0:T(8,128)(2,1)}), bf16[16,464,320]{1,2,0:T(8,128)(2,1)}) %all-gather.8.cloned.1.call-update) | async-done | bytes 4751376 | tf_op jit(solution)/shard_map/all_gather | solution.py:48
  69.0 7.8 %copy.39 = bf16[16,464,320]{1,0,2:T(8,128)(2,1)} copy(bf16[16,464,320]{1,2,0:T(8,128)(2,1)} %all-gather.8.cloned.1.call-done) | data formatting | bytes 9502720 | tf_op jit(solution)/shard_map/all_gather | solution.py:48
  76.8 11.1 %reshape.128 = bf16[7424,320]{0,1:T(8,128)(2,1)} reshape(bf16[16,464,320]{1,0,2:T(8,128)(2,1)} %copy.39) | data formatting | bytes 9502720
  89.3 0.6 fusion.48
  90.5 0.3 dynamic-update-slice.1
  90.8 0.2 dynamic-update-slice
  91.0 59.3 %all-reduce.7 = (bf16[7424]{0:T(1024)(128)(2,1)S(1)}, bf16[7424]{0:T(1024)(128)(2,1)S(1)}) all-reduce(bf16[7424]{0:T(1024)(128)(2,1)S(1)} %dynamic-update-slice.1, bf16[7424]{0:T(1024)(128)(2,1)S(1)} %dynamic-update-slice), channel_id=1, replica_groups=mesh['node'=16,'local'=2] {'node'}, use_global_device_ids=true, to_apply=%add.1 | all-reduce | flops 14848 | bytes 59392
  150.3 5.3 %all-gather.1 = bf16[2,1,7424]{2,1,0:T(2,128)(2,1)S(1)} all-gather(bf16[1,1,7424]{2,1,0:T(2,128)(2,1)S(1)} %reshape.125), channel_id=1, replica_groups=mesh['node'=16,'local'=2] {'local'}, dimensions={0}, use_global_device_ids=true | all-gather | bytes 44544 | tf_op jit(solution)/shard_map/all_gather | solution.py:55
  155.6 0.2 convert_reduce_fusion.1
  155.9 5.3 %all-gather = bf16[2,1,7424]{2,1,0:T(2,128)(2,1)S(1)} all-gather(bf16[1,1,7424]{2,1,0:T(2,128)(2,1)S(1)} %reshape.123), channel_id=1, replica_groups=mesh['node'=16,'local'=2] {'local'}, dimensions={0}, use_global_device_ids=true | all-gather | bytes 44544 | tf_op jit(solution)/shard_map/all_gather | solution.py:54
  161.2 0.2 convert_reduce_fusion.2
  161.4 0.6 select_reduce_fusion
  162.1 0.7 convert_multiply_fusion
  162.7 0.1 copy.44
  162.9 3.5 convert_reduce_fusion
  166.4 4.3 fusion.14
  170.7 0.1 fusion.26
  170.8 0.4 multiply_cosine_fusion
  171.3 35.3 %all-gather.6.cloned.1.call-done = bf16[14848,320]{0,1:T(8,128)(2,1)} async-done(((bf16[7424,320]{0,1:T(8,128)(2,1)}), bf16[14848,320]{0,1:T(8,128)(2,1)}) %all-gather.6.cloned.1.call-update) | async-done | bytes 9502736 | tf_op jit(solution)/shard_map/all_gather | solution.py:53
  206.6 9.3 %fusion.45 = f32[192,320]{1,0:T(8,128)S(1)} fusion(bf16[14848,320]{0,1:T(8,128)(2,1)} %all-gather.6.cloned.1.call-done, bf16[192,14848]{1,0:T(8,128)(2,1)} %param.8, f32[14848]{0:T(1024)S(1)} %reshape.130, f32[14848]{0:T(1024)S(1)} %reshape.129, f32[192]{0:T(256)S(1)} %add_rsqrt_fusion, f32[192]{0:T(256)S(1)} %broadcast_multiply_fusion.2), kind=kOutput, calls=%fused_computation.95 | convolution fusion | flops 1841627136 | bytes 15570432 | tf_op jit(solution)/shard_map/dot_general | solution.py:59
  216.2 0.2 fusion.34
  216.5 4.8 all_gather.28
  221.5 0.6 fusion.49
  222.1 0.2 fusion.25
  222.2 0.4 fusion.24
  222.6 0.4 convolution_bitcast_fusion.1
  223.0 0.4 fusion.22
  223.5 0.3 convolution_bitcast_fusion.3
  223.8 0.4 convolution_bitcast_fusion.2
  224.1 0.8 pad_maximum_fusion
  225.0 0.3 reduce-scatter.8.cloned.1.call-start
  225.3 10.7 %reduce-scatter.6.cloned.1.call-done = f32[192,128]{1,0:T(8,128)} async-done(((f32[384,128]{1,0:T(8,128)}), f32[192,128]{1,0:T(8,128)}) %reduce-scatter.6.cloned.1.call-update) | async-done | bytes 98320 | tf_op jit(solution)/shard_map/reduce_scatter | solution.py:103
  236.1 1.0 slice.103
  237.1 0.9 slice_bitcast_fusion.4
  238.1 1.1 fusion.36
  239.3 9.2 %convolution_convert_fusion = bf16[14848,320]{0,1:T(8,128)(2,1)} fusion(bf16[192,64]{0,1:T(8,128)(2,1)S(1)} %copy.51, bf16[192,64]{0,1:T(8,128)(2,1)S(1)} %copy.50, bf16[192,192]{0,1:T(8,128)(2,1)S(1)} %bitcast.90, bf16[192,14848]{1,0:T(8,128)(2,1)} %param.8, f32[14848]{0:T(1024)S(1)} %reshape.130, f32[14848]{0:T(1024)S(1)} %reshape.129, ...), kind=kOutput, calls=%fused_computation.1 | convolution fusion | flops 1846747136 | bytes 15447552 | tf_op jit(solution)/shard_map/dot_general | solution.py:127
  248.5 111.4 %reduce-scatter.8.cloned.1.call-done = bf16[7424,320]{0,1:T(8,128)(2,1)} async-done(((bf16[14848,320]{0,1:T(8,128)(2,1)}), bf16[7424,320]{0,1:T(8,128)(2,1)}) %reduce-scatter.8.cloned.1.call-update) | async-done | bytes 4751376 | tf_op jit(solution)/shard_map/reduce_scatter | solution.py:133
  359.9 8.4 %copy.64 = f32[7424,320]{1,0:T(8,128)} copy(bf16[7424,320]{0,1:T(8,128)(2,1)} %reduce-scatter.8.cloned.1.call-done) | data formatting | bytes 14254080
  368.3 0.6 dynamic-slice.2
  370.2 12.5 %fusion.13 = (bf16[14848]{0:T(1024)(128)(2,1)S(1)}, f32[192]{0:T(256)S(1)}, f32[192]{0:T(256)S(1)}, bf16[14848]{0:T(1024)(128)(2,1)S(1)}, f32[192,14848]{1,0:T(8,128)}) fusion(bf16[192,14848]{1,0:T(8,128)(2,1)} %param.8, f32[192]{0:T(256)S(1)} %add_rsqrt_fusion, f32[192]{0:T(256)S(1)} %broadcast_multiply_fusion.2, f32[14848]{0:T(1024)S(1)} %reshape.129, ...), kind=kOutput, calls=%fused_computation.16 | convolution fusion | flops 1853368832 | bytes 26852352 | tf_op jit(solution)/shard_map/dot_general | solution.py:115
  382.7 7.7 %all-reduce.8 = (bf16[14848]{0:T(1024)(128)(2,1)S(1)}, bf16[14848]{0:T(1024)(128)(2,1)S(1)}) all-reduce(bf16[14848]{0:T(1024)(128)(2,1)S(1)} %get-tuple-element.4, bf16[14848]{0:T(1024)(128)(2,1)S(1)} %get-tuple-element.7), channel_id=5, replica_groups=mesh['node'=16,'local'=2] {'local'}, use_global_device_ids=true, to_apply=%region_12.13.clone | all-reduce | flops 29696 | bytes 118784
  390.6 63.2 %all-reduce.6 = (f32[7424]{0:T(1024)S(1)}, f32[7424]{0:T(1024)S(1)}) all-reduce(f32[7424]{0:T(1024)S(1)} %get-tuple-element.35, f32[7424]{0:T(1024)S(1)} %get-tuple-element.34), channel_id=6, replica_groups=mesh['node'=16,'local'=2] {'node'}, use_global_device_ids=true, to_apply=%region_13.14.clone | all-reduce | flops 14848 | bytes 118784
  453.7 0.7 dynamic-slice.5
  454.4 0.7 dynamic-slice.9
  455.0 10.4 %fusion.12 = bf16[192,14848]{1,0:T(8,128)(2,1)} fusion(bf16[192,14848]{1,0:T(8,128)(2,1)} %param.8, f32[192,14848]{1,0:T(8,128)} %get-tuple-element.31, f32[192]{0:T(256)S(1)} %get-tuple-element.32, f32[192]{0:T(256)S(1)} %get-tuple-element.33, f32[14848]{0:T(1024)S(1)} %reshape.129, f32[192]{0:T(256)S(1)} %add_rsqrt_fusion, f32[192]{0:T(256)S(1)} %broadcast_multiply_fusion.2), kind=kLoop, calls=%fused_computation.15 | loop fusion | flops 25657344 | bytes 22868992 | tf_op jit(solution)/shard_map/convert_element_type | solution.py:148
  465.4 30.5 %reduce-scatter.10.cloned.1.call-done = f32[464,320]{1,0:T(8,128)} async-done(((f32[7424,320]{1,0:T(8,128)}), f32[464,320]{1,0:T(8,128)}) %reduce-scatter.10.cloned.1.call-update) | async-done | bytes 593936
  496.0 2.2 copy.65
  (51 shorter events, 1.5 us)
Async XLA Ops:
  7.2 61.8 %all-gather.8.cloned.1.call-start = ((), (), s32[]{:S(2)}) async-start(), calls=%async_computation.6 | async-start | bytes 5570560 | tf_op jit(solution)/shard_map/all_gather | solution.py:48
  7.9 81.3 %copy-start.2 = (u32[32]{0:T(128)S(1)}, u32[32]{0:T(128)}, u32[]{:S(2)}) copy-start(u32[32]{0:T(128)} %constant.36) | copy-start | bytes 388
  7.9 82.6 %copy-start.3 = (bf16[464]{0:T(512)(128)(2,1)S(1)}, bf16[464]{0:T(512)(128)(2,1)}, u32[]{:S(2)}) copy-start(bf16[464]{0:T(512)(128)(2,1)} %param.12) | copy-start | bytes 2788
  7.9 82.9 %copy-start.4 = (bf16[464]{0:T(512)(128)(2,1)S(1)}, bf16[464]{0:T(512)(128)(2,1)}, u32[]{:S(2)}) copy-start(bf16[464]{0:T(512)(128)(2,1)} %param.11) | copy-start | bytes 2788
  7.9 153.5 %copy-start.1 = (f32[8192]{0:T(1024)S(1)}, f32[8192]{0:T(1024)}, u32[]{:S(2)}) copy-start(f32[8192]{0:T(1024)} %param.15) | copy-start | bytes 98308
  7.9 154.1 %copy-start = (bf16[192,192]{1,0:T(8,128)(2,1)S(1)}, bf16[192,192]{1,0:T(8,128)(2,1)}, u32[]{:S(2)}) copy-start(bf16[192,192]{1,0:T(8,128)(2,1)} %param.9) | copy-start | bytes 221188
  8.0 198.6 %all-gather.6.cloned.1.call-start = ((), (), s32[]{:S(2)}) async-start(), calls=%async_computation.3 | async-start | bytes 14254080 | tf_op jit(solution)/shard_map/all_gather | solution.py:53
  87.9 148.2 %reduce-scatter.6.cloned.1.call-start = ((), (), s32[]{:S(2)}) async-start(), calls=%async_computation.4 | async-start | bytes 294912 | tf_op jit(solution)/shard_map/reduce_scatter | solution.py:103
  225.0 134.9 %reduce-scatter.8.cloned.1.call-start = ((), (), s32[]{:S(2)}) async-start(), calls=%async_computation.5 | async-start | bytes 14254080 | tf_op jit(solution)/shard_map/reduce_scatter | solution.py:133
  248.5 119.9 %copy-start.5 = (u32[32]{0:T(128)S(1)}, u32[32]{0:T(128)}, u32[]{:S(2)}) copy-start(u32[32]{0:T(128)} %constant.48) | copy-start | bytes 388
  248.5 247.5 %reduce-scatter.10.cloned.1.call-start = ((), (), s32[]{:S(2)}) async-start(), calls=%async_computation.7 | async-start | bytes 12115968
Sparse Core Ops, SparseCore 0:
  10.3 58.6 all-gather.7
  88.0 118.5 all-gather.5
  225.1 10.9 reduce-scatter.5
  248.6 111.2 reduce-scatter.7
  368.4 127.4 reduce-scatter.9
where the time goes:
time: 506 us; the launch traced here: 505 us
  waiting for transfers between devices  250 us (49%)
  blocking collectives  146 us (29%)
  local copies, waits for them, and re-layouts  35.2 us (7%)
  matrix products  33.4 us (7%)
  other arithmetic  23 us (5%)
  between operations  17.4 us (3%)
    unnamed x3, blocking collectives  130 us
    reduce_scatter x1, waiting for transfers between devices, on_device(): lax.psum_scatter(term_weight.astype(jnp.bfloat16), 'local', scatter_dimen...  111 us
    all_gather x1, waiting for transfers between devices, on_device(): lax.all_gather(w_qkv, 'node', axis=0, tiled=True)  61 us
    all_gather x1, waiting for transfers between devices, on_device(): w_piece = lax.all_gather(w_second, 'local', axis=0, tiled=True)  35.3 us
    unnamed x6, waiting for transfers between devices  31.3 us
    unnamed x25, local copies, waits for them, and re-layouts  24.7 us
    dot_general x1, matrix products, on_device(): lax.dot_general(d_projected, lax.all_gather(w_second, 'local', axis=0, ti...  12.5 us
    reduce_scatter x1, waiting for transfers between devices, on_device(): lax.psum_scatter(jnp.concatenate([d_key_term, d_value_term], axis=1), 'lo...  10.7 us
  transfers between devices with their start and end apart: 5, of which 5 were waited for; matrix products, arithmetic and copies ran while one was open for 7% of the time, Pallas kernels for 0%

commit v1 on v0

v1 whole, which is shorter than its diff:
```python
import functools

import jax
import jax.numpy as jnp
from jax import lax
from jax.experimental import pallas as pl
from jax.experimental.pallas import tpu as pltpu
from jax.sharding import PartitionSpec as P

HD = 64
QH = 3
LANES = 384
MESH = pl.DeviceIdType.MESH


epsilon = 1e-05


def rope_tables(positions, head_size):
    half_size = head_size // 2
    steps = 2.0 * jnp.arange(half_size, dtype=jnp.float32) / head_size
    freqs = jnp.exp(-jnp.log(10000.0) * steps)
    angles = positions.astype(jnp.float32)[:, None] * freqs[None, :]
    cosine = jnp.concatenate([jnp.cos(angles), jnp.cos(angles)], axis=1)
    sine_table = jnp.concatenate([jnp.sin(angles), jnp.sin(angles)], axis=1)
    return (cosine, sine_table)


def rotate(values, cosine, sine_table):
    half_size = values.shape[-1] // 2
    turned = jnp.concatenate([-values[..., half_size:], values[..., :half_size]], axis=-1)
    return values * cosine[:, None, :] + turned * sine_table[:, None, :]


def unrotate(values, cosine, sine_table):
    half_size = values.shape[-1] // 2
    turned = jnp.concatenate([values[..., half_size:], -values[..., :half_size]], axis=-1)
    return values * cosine[:, None, :] + turned * sine_table[:, None, :]


def place(Z, L):
    node = lax.axis_index("node")
    z, x, c = node // 4, (node // 2) % 2, node % 2
    q = lax.axis_index("local") * 2 + x
    return z, q, c


def device(z, q, c):
    return (z * 4 + (q % 2) * 2 + c, q // 2)


def greet(Z, Q, z, q, c):
    barrier = pltpu.get_barrier_semaphore()

    def tell(target):
        pl.semaphore_signal(barrier, inc=1, device_id=target, device_id_type=MESH)

    tell(device(z, q, 1 - c))
    for d in range(1, Z):
        tell(device((z + d) % Z, q, c))
    for d in range(1, Q):
        tell(device(z, (q + d) % Q, c))
    pl.semaphore_wait(barrier, Z + Q - 1)


def gather_kernel(Z, L, own, out, local_sem, send_z, send_q, send_c, recv, recv_c):
    Q = 2 * L
    z, q, c = place(Z, L)
    greet(Z, Q, z, q, c)

    def remote(src, zz, qq, send, got, target):
        return pltpu.make_async_remote_copy(
            src_ref=src,
            dst_ref=out.at[qq, zz, c],
            send_sem=send,
            recv_sem=got,
            device_id=target,
            device_id_type=MESH,
        )

    mine = pltpu.make_async_copy(own, out.at[q, z, c], local_sem)
    mine.start()

    def to_z(d):
        return remote(own, z, q, send_z.at[d - 1], recv.at[q, z], device((z + d) % Z, q, c))

    def to_q(k, d, src):
        zz = (z + Z - k) % Z
        return remote(src, zz, q, send_q.at[k, d - 1], recv.at[q, zz], device(z, (q + d) % Q, c))

    def to_c(zz, qq, src):
        return remote(src, zz, qq, send_c.at[qq, zz], recv_c.at[qq, zz], device(z, q, 1 - c))

    def landed(zz, qq):
        pltpu.make_async_copy(own, out.at[qq, zz, c], recv.at[qq, zz]).wait()

    for d in range(1, Z):
        to_z(d).start()
    for d in range(1, Q):
        to_q(0, d, own).start()
    to_c(z, q, own).start()

    def spread(k, carry):
        zz = (z + Z - k) % Z
        landed(zz, q)
        for d in range(1, Q):
            to_q(k, d, out.at[q, zz, c]).start()
        to_c(zz, q, out.at[q, zz, c]).start()
        return carry

    lax.fori_loop(1, Z, spread, 0)

    def forward(k, carry):
        zz = (z + Z - k) % Z
        for d in range(1, Q):
            qq = (q + d) % Q
            landed(zz, qq)
            to_c(zz, qq, out.at[qq, zz, c]).start()
        return carry

    lax.fori_loop(0, Z, forward, 0)

    mine.wait()
    for d in range(1, Z):
        to_z(d).wait_send()

    def finish(k, carry):
        for d in range(1, Q):
            to_q(k, d, own).wait_send()
        for d in range(Q):
            to_c(k, (q + d) % Q, own).wait_send()
            pltpu.make_async_copy(
                own, out.at[(q + d) % Q, k, 1 - c], recv_c.at[(q + d) % Q, k]
            ).wait()
        return carry

    lax.fori_loop(0, Z, finish, 0)


def gather(block, Z, L):
    rows = block.shape[0]
    Q = 2 * L
    return pl.pallas_call(
        functools.partial(gather_kernel, Z, L),
        out_shape=jax.ShapeDtypeStruct((Q, Z, 2, rows, LANES), jnp.bfloat16),
        in_specs=[pl.BlockSpec(memory_space=pl.ANY)],
        out_specs=pl.BlockSpec(memory_space=pl.ANY),
        scratch_shapes=[
            pltpu.SemaphoreType.DMA,
            pltpu.SemaphoreType.DMA((max(Z - 1, 1),)),
            pltpu.SemaphoreType.DMA((Z, Q - 1)),
            pltpu.SemaphoreType.DMA((Q, Z)),
            pltpu.SemaphoreType.DMA((Q, Z)),
            pltpu.SemaphoreType.DMA((Q, Z)),
        ],
        compiler_params=pltpu.CompilerParams(collective_id=0, has_side_effects=True),
    )(block)


def scatter_kernel(
    Z, L, part, out, own, pair, plane, tall, column,
    sem_own, send_c, recv_c, send_q, recv_q, send_z, recv_z,
):
    Q = 2 * L
    z, q, c = place(Z, L)
    greet(Z, Q, z, q, c)

    def load(zz, qq):
        return pltpu.make_async_copy(part.at[qq, zz, c], own.at[qq, zz], sem_own.at[qq, zz])

    def to_c(zz, qq):
        return pltpu.make_async_remote_copy(
            src_ref=part.at[qq, zz, 1 - c],
            dst_ref=pair.at[qq, zz],
            send_sem=send_c.at[qq, zz],
            recv_sem=recv_c.at[qq, zz],
            device_id=device(z, q, 1 - c),
            device_id_type=MESH,
        )

    def to_q(zz, qq):
        return pltpu.make_async_remote_copy(
            src_ref=own.at[qq, zz],
            dst_ref=plane.at[zz, q],
            send_sem=send_q.at[qq, zz],
            recv_sem=recv_q.at[zz, q],
            device_id=device(z, qq, c),
            device_id_type=MESH,
        )

    def to_z(zz):
        return pltpu.make_async_remote_copy(
            src_ref=tall.at[zz],
            dst_ref=column.at[z],
            send_sem=send_z.at[zz],
            recv_sem=recv_z.at[z],
            device_id=device(zz, q, c),
            device_id_type=MESH,
        )

    def begin(k, carry):
        zz = (z + k) % Z
        for d in range(Q):
            qq = (q + d + 1) % Q
            to_c(zz, qq).start()
            load(zz, qq).start()
        return carry

    lax.fori_loop(1, Z + 1, begin, 0)

    def join(zz, qq):
        load(zz, qq).wait()
        to_c(zz, qq).wait_recv()
        total = own[qq, zz].astype(jnp.float32) + pair[qq, zz].astype(jnp.float32)
        own[qq, zz] = total.astype(jnp.bfloat16)

    def pairs(k, carry):
        zz = (z + k) % Z

        def one(d, carry):
            qq = (q + d) % Q
            join(zz, qq)
            to_q(zz, qq).start()
            return carry

        lax.fori_loop(1, Q, one, 0)
        join(zz, q)
        return carry

    lax.fori_loop(1, Z + 1, pairs, 0)

    def plane_sum(zz):
        tall[zz] = own[q, zz].astype(jnp.float32)

        def add(d, carry):
            qq = (q + d) % Q
            pltpu.make_async_copy(own.at[qq, zz], plane.at[zz, qq], recv_q.at[zz, qq]).wait()
            tall[zz] += plane[zz, qq].astype(jnp.float32)
            return carry

        lax.fori_loop(1, Q, add, 0)

    def columns(k, carry):
        zz = (z + k) % Z
        plane_sum(zz)
        to_z(zz).start()
        return carry

    lax.fori_loop(1, Z, columns, 0)
    plane_sum(z)
    out[...] = tall[z]

    def last(k, carry):
        zz = (z + Z - k) % Z
        pltpu.make_async_copy(tall.at[zz], column.at[zz], recv_z.at[zz]).wait()
        out[...] += column[zz]
        return carry

    lax.fori_loop(1, Z, last, 0)

    def finish(k, carry):
        zz = (z + k) % Z
        for d in range(Q):
            to_c(zz, (q + d) % Q).wait_send()
        for d in range(1, Q):
            to_q(zz, (q + d) % Q).wait_send()
        return carry

    lax.fori_loop(0, Z, finish, 0)
    for d in range(1, Z):
        to_z((z + d) % Z).wait_send()


def scatter_sum(part, Z, L):
    rows = part.shape[-2]
    Q = 2 * L
    dma = pltpu.SemaphoreType.DMA
    return pl.pallas_call(
        functools.partial(scatter_kernel, Z, L),
        out_shape=jax.ShapeDtypeStruct((rows, LANES), jnp.float32),
        in_specs=[pl.BlockSpec(memory_space=pl.ANY)],
        out_specs=pl.BlockSpec(memory_space=pltpu.VMEM),
        scratch_shapes=[
            pltpu.VMEM((Q, Z, rows, LANES), jnp.bfloat16),
            pltpu.VMEM((Q, Z, rows, LANES), jnp.bfloat16),
            pltpu.VMEM((Z, Q, rows, LANES), jnp.bfloat16),
            pltpu.VMEM((Z, rows, LANES), jnp.float32),
            pltpu.VMEM((Z, rows, LANES), jnp.float32),
            dma((Q, Z)),
            dma((Q, Z)),
            dma((Q, Z)),
            dma((Q, Z)),
            dma((Z, Q)),
            dma((Z,)),
            dma((Z,)),
        ],
        compiler_params=pltpu.CompilerParams(
            collective_id=1, has_side_effects=True, vmem_limit_bytes=44 * 2**20
        ),
    )(part)


def on_device(
    Z, L, hidden_in, grad_heads, w_qkv, ln_gain, ln_bias, seq_lengths, sample_index, priority
):
    tok_rows, model_width = hidden_in.shape
    shard, qkv = w_qkv.shape
    padded = -(-shard // 16) * 16
    query_cols = QH * HD

    def whole(blocks):
        blocks = blocks[:, :, :, :shard]
        blocks = blocks.reshape((L, 2, Z, 2) + blocks.shape[3:])
        return blocks.transpose(0, 2, 1, 3, 4, 5).reshape(model_width, -1)

    def apart(rows):
        blocks = rows.reshape(L, Z, 2, 2, shard, -1).transpose(0, 2, 1, 3, 4, 5)
        blocks = blocks.reshape(2 * L, Z, 2, shard, -1)
        return jnp.pad(blocks, ((0, 0), (0, 0), (0, 0), (0, padded - shard), (0, 0)))

    own_block = jnp.concatenate([w_qkv, ln_gain[:, None], ln_bias[:, None]], axis=1)
    own_block = jnp.pad(own_block, ((0, padded - shard), (0, LANES - qkv - 2)))
    w_all = whole(gather(own_block, Z, L))
    picks = jnp.arange(16)[:, None] + qkv == jnp.arange(LANES)[None, :]
    picks = (picks & (jnp.arange(16) < 2)[:, None]).astype(jnp.bfloat16)
    contract = (((1,), (1,)), ((), ()))
    rows = lax.dot_general(picks, w_all, contract, preferred_element_type=jnp.float32)
    gain, bias = rows[0:1], rows[1:2]
    values = hidden_in.astype(jnp.float32)
    centre = jnp.mean(values, axis=-1, keepdims=True)
    shifted = values - centre
    variance = jnp.mean(shifted * shifted, axis=-1, keepdims=True)
    inverse = lax.rsqrt(variance + epsilon)
    normalized = shifted * inverse
    normed = (normalized * gain + bias).astype(jnp.bfloat16)
    proj_total = jnp.dot(normed, w_all, preferred_element_type=jnp.float32)[:, :qkv]
    positions = lax.axis_index("local") * tok_rows + jnp.arange(tok_rows, dtype=jnp.int32)
    cosine, sine_table = rope_tables(positions, HD)
    query = rotate(proj_total[:, :query_cols].reshape(tok_rows, QH, HD), cosine, sine_table).astype(
        jnp.bfloat16
    )
    keys_own = rotate(proj_total[:, query_cols : query_cols + HD][:, None, :], cosine, sine_table)[
        :, 0, :
    ]
    pair_own = jnp.concatenate([keys_own, proj_total[:, query_cols + HD :]], axis=1).astype(
        jnp.bfloat16
    )
    pair_all = lax.all_gather(pair_own, "local", axis=0, tiled=True)
    seq_rows = pair_all.shape[0]
    keys_all = pair_all[:, :HD]
    values_all = pair_all[:, HD:]
    length = seq_lengths[0]
    weight = lax.dynamic_slice(priority, (sample_index[0],), (1,))[0]
    scale = HD ** (-0.5)
    scores = jnp.einsum("qhd,kd->hqk", query, keys_all, preferred_element_type=jnp.float32) * scale
    key_positions = jnp.arange(seq_rows, dtype=jnp.int32)
    allowed = (key_positions[None, :] <= positions[:, None]) & (key_positions[None, :] < length)
    scores = jnp.where(allowed[None], scores, -1e30)
    row_max = jnp.max(scores, axis=-1, keepdims=True)
    exponent = jnp.exp(scores - row_max)
    attention = exponent / jnp.sum(exponent, axis=-1, keepdims=True)
    attention_b = attention.astype(jnp.bfloat16)
    head_out = jnp.einsum(
        "hqk,kd->qhd", attention_b, values_all, preferred_element_type=jnp.float32
    )
    live_rows = (positions < length).astype(jnp.float32)
    cotangent = (
        grad_heads.reshape(tok_rows, QH, HD).astype(jnp.float32) * weight * live_rows[:, None, None]
    ).astype(jnp.bfloat16)
    d_attention = jnp.einsum(
        "qhd,kd->hqk", cotangent, values_all, preferred_element_type=jnp.float32
    )
    row_delta = jnp.sum(cotangent.astype(jnp.float32) * head_out, axis=-1)
    d_scores = (attention * (d_attention - row_delta.T[:, :, None]) * scale).astype(jnp.bfloat16)
    d_query = jnp.einsum("hqk,kd->qhd", d_scores, keys_all, preferred_element_type=jnp.float32)
    d_key_term = jnp.einsum("hqk,qhd->kd", d_scores, query, preferred_element_type=jnp.float32)
    d_value_term = jnp.einsum(
        "hqk,qhd->kd", attention_b, cotangent, preferred_element_type=jnp.float32
    )
    d_pair = lax.psum_scatter(
        jnp.concatenate([d_key_term, d_value_term], axis=1),
        "local",
        scatter_dimension=0,
        tiled=True,
    )
    d_query_pre = unrotate(d_query, cosine, sine_table).reshape(tok_rows, query_cols)
    d_key_pre = unrotate(d_pair[:, None, :HD], cosine, sine_table)[:, 0, :]
    d_projected = jnp.concatenate([d_query_pre, d_key_pre, d_pair[:, HD:]], axis=1)
    d_projected = jnp.pad(d_projected.astype(jnp.bfloat16), ((0, 0), (0, LANES - qkv)))
    d_normed = lax.dot_general(d_projected, w_all, contract, preferred_element_type=jnp.float32)
    grad_hat = d_normed * gain
    grad_input = inverse * (
        grad_hat
        - jnp.mean(grad_hat, axis=-1, keepdims=True)
        - normalized * jnp.mean(grad_hat * normalized, axis=-1, keepdims=True)
    )
    term_gain = jnp.sum(d_normed * normalized, axis=0, keepdims=True).astype(jnp.bfloat16)
    term_bias = jnp.sum(d_normed, axis=0, keepdims=True).astype(jnp.bfloat16)
    left = jnp.concatenate(
        [normed, term_gain, term_bias, jnp.zeros((14, model_width), jnp.bfloat16)], axis=0
    )
    right = jnp.concatenate([d_projected, picks], axis=0)
    term = lax.dot_general(
        left, right, (((0,), (0,)), ((), ())), preferred_element_type=jnp.float32
    ).astype(jnp.bfloat16)
    totals = scatter_sum(apart(term), Z, L)[:shard]
    return (
        grad_input.astype(jnp.bfloat16),
        totals[:, :qkv],
        totals[:, qkv],
        totals[:, qkv + 1],
    )


def solution(mesh):
    Z, L = mesh.shape["node"] // 4, mesh.shape["local"]
    return jax.shard_map(
        functools.partial(on_device, Z, L),
        mesh=mesh,
        in_specs=(
            P(("node", "local"), None),
            P(("node", "local"), None),
            P(("local", "node"), None),
            P(("local", "node")),
            P(("local", "node")),
            P("node"),
            P("node"),
            P(),
        ),
        out_specs=(
            P(("node", "local"), None),
            P(("local", "node"), None),
            P(("local", "node")),
            P(("local", "node")),
        ),
        check_vma=False,
    )
```

time: 506 us -> 269 us (0.53)
  waiting for transfers between devices: 250 us -> 10.2 us
  Pallas kernels: 0 us -> 159 us
  blocking collectives: 146 us -> 4.96 us
  local copies, waits for them, and re-layouts: 35.2 us -> 22.5 us
    pallas_call x0 -> x2, Pallas kernels: none -> 159 us  [the longest x1 86.8 us: scatter_sum(): pl.pallas_call(functools.partial(scatter_kernel, Z, L), out_shape=jax.Sha...]
    unnamed x3 -> x0, blocking collectives: 130 us -> none
    reduce_scatter x1 -> x0, waiting for transfers between devices: 111 us -> none  [on_device(): lax.psum_scatter(term_weight.astype(jnp.bfloat16), 'local', scatter_dimen...]
    all_gather x2 -> x0, waiting for transfers between devices: 96.3 us -> none  [the longest x1 61 us: on_device(): lax.all_gather(w_qkv, 'node', axis=0, tiled=True)]
    unnamed x6 -> x1, waiting for transfers between devices: 31.3 us -> 0.02 us
    unnamed x25 -> x20, local copies, waits for them, and re-layouts: 24.7 us -> 4.73 us
    reshape x0 -> x2, local copies, waits for them, and re-layouts: none -> 12.2 us  [the longest x1 6.43 us: whole(): blocks = blocks.reshape((L, 2, Z, 2) + blocks.shape[3:])]
    all_gather x2 -> x0, blocking collectives: 10.6 us -> none  [the longest x1 5.34 us: on_device(): gain_piece = lax.all_gather(gain_second, 'local', axis=0, tiled=True)]
  transfers between devices with their start and end apart: 5 -> 1, of which waited for: 5 -> 1; matrix products, arithmetic and copies ran while one was open for 7% -> 0% of each run, Pallas kernels for 0% -> 0%
where the time goes in v1:
time: 269 us
  Pallas kernels  159 us (59%)
  matrix products  28.5 us (11%)
  other arithmetic  27.8 us (10%)
  local copies, waits for them, and re-layouts  22.5 us (8%)
  between operations  15.8 us (6%)
  waiting for transfers between devices  10.2 us (4%)
  blocking collectives  4.96 us (2%)
    pallas_call x1, Pallas kernels, scatter_sum(): pl.pallas_call(functools.partial(scatter_kernel, Z, L), out_shape=jax.Sha...  86.8 us
    pallas_call x1, Pallas kernels, gather(): pl.pallas_call(functools.partial(gather_kernel, Z, L), out_shape=jax.Shap...  71.9 us
    dot_general x1, matrix products, on_device(): lax.dot_general(d_projected, w_all, contract, preferred_element_type=jnp....  13 us
    convert_element_type x1, other arithmetic, on_device(): grad_input.astype(jnp.bfloat16)  10.3 us
    reduce_scatter x1, waiting for transfers between devices, on_device(): lax.psum_scatter(jnp.concatenate([d_key_term, d_value_term], axis=1), 'lo...  10.2 us
    reshape x1, local copies, waits for them, and re-layouts, whole(): blocks = blocks.reshape((L, 2, Z, 2) + blocks.shape[3:])  6.43 us
    reshape x1, local copies, waits for them, and re-layouts, apart(): blocks = rows.reshape(L, Z, 2, 2, shard, -1).transpose(0, 2, 1, 3, 4, 5)  5.78 us
  transfers between devices with their start and end apart: 1, of which 1 were waited for; matrix products, arithmetic and copies ran while one was open for 0% of the time, Pallas kernels for 0%

profile of v1, /device:TPU:0, one launch (start us, length us, event | category | flops | bytes accessed | tf_op | source)
XLA Modules:
  0.0 268.5 jit_solution(17394460609669997672)
XLA Ops:
  7.3 3.5 %convert_reduce_fusion = f32[192]{0:T(256)S(1)} fusion(bf16[192,14848]{1,0:T(8,128)(2,1)} %param.8), kind=kLoop, calls=%fused_computation.3 | loop fusion | flops 5701440 | bytes 5702400 | tf_op jit(solution)/shard_map/reduce_sum | solution.py:330
  10.8 4.3 %fusion.14 = f32[192]{0:T(256)S(1)} fusion(bf16[192,14848]{1,0:T(8,128)(2,1)} %param.8, f32[192]{0:T(256)S(1)} %broadcast_multiply_fusion.2), kind=kLoop, calls=%fused_computation.17 | loop fusion | flops 11403072 | bytes 5703168 | tf_op jit(solution)/shard_map/reduce_sum | solution.py:332
  15.1 0.1 broadcast_in_dim.30
  15.2 0.1 broadcast_in_dim.29
  15.4 0.2 copy.29
  15.6 0.9 fusion.40.own
  16.5 71.9 %shard_map.111 = bf16[4,4,2,464,384]{4,3,2,1,0:T(8,128)(2,1)} custom-call(bf16[464,384]{1,0:T(8,128)(2,1)} %fusion.40.own), custom_call_target="tpu_custom_call" | custom-call | tf_op jit(solution)/shard_map/pallas_call | solution.py:143
  88.4 6.4 %copy.32 = bf16[2,2,4,2,464,384]{5,4,3,1,2,0:T(8,128)(2,1)S(1)} copy(bf16[2,2,4,2,464,384]{5,4,3,2,1,0:T(8,128)(2,1)} %bitcast.99) | data formatting | bytes 22806528 | tf_op jit(solution)/shard_map/reshape | solution.py:313
  94.9 3.0 %fusion.60 = f32[16,14848]{1,0:T(8,128)S(1)} fusion(bf16[14848,384]{1,0:T(8,128)(2,1)S(1)} %bitcast.96, s32[16]{0:T(128)S(1)} %iota_add_fusion.1, pred[16]{0:T(512)(128)(4,1)S(1)} %iota_compare_fusion.5), kind=kOutput, calls=%fused_computation.103 | convolution fusion | flops 182470656 | bytes 12353616 | tf_op jit(solution)/shard_map/dot_general | solution.py:327
  97.9 0.3 slice_reduce_fusion.3
  98.3 1.9 slice-done
  100.2 1.4 slice-done.1
  101.6 4.9 %fusion.8 = bf16[192,14848]{1,0:T(8,128)(2,1)} fusion(bf16[192,14848]{1,0:T(8,128)(2,1)S(1)} %bitcast.95, f32[14848]{0:T(1024)S(1)} %get-tuple-element.17, f32[14848]{0:T(1024)S(1)} %get-tuple-element.16, f32[192]{0:T(256)S(1)} %add_rsqrt_fusion, f32[192]{0:T(256)S(1)} %broadcast_multiply_fusion.2), kind=kLoop, calls=%fused_computation.11 | loop fusion | flops 17104896 | bytes 11523584 | tf_op jit(solution)/shard_map/convert_element_type | solution.py:335
  106.5 5.3 %fusion.70 = f32[192,384]{1,0:T(8,128)S(1)} fusion(bf16[192,14848]{1,0:T(8,128)(2,1)} %fusion.8, bf16[14848,384]{1,0:T(8,128)(2,1)S(1)} %bitcast.97), kind=kOutput, calls=%fused_computation.121 | convolution fusion | flops 2189426688 | bytes 17399808 | tf_op jit(solution)/shard_map/dot_general | solution.py:336
  111.9 0.1 slice_bitcast_fusion.5
  112.0 0.1 copy.33
  112.2 0.1 fusion.54
  112.3 0.4 multiply_cosine_fusion
  112.7 0.2 fusion.56
  112.9 0.1 copy.35
  113.7 0.1 pad_maximum_fusion.3
  113.8 5.0 %all_gather.3 = bf16[384,128]{1,0:T(8,128)(2,1)S(1)} all-gather(bf16[192,128]{1,0:T(8,128)(2,1)S(1)} %pad_maximum_fusion.3), channel_id=1, replica_groups=mesh['node'=16,'local'=2] {'local'}, dimensions={0}, use_global_device_ids=true | all-gather | bytes 147456 | tf_op jit(solution)/shard_map/all_gather | solution.py:348
  119.4 1.3 dynamic_slice.3
  120.7 0.7 convert_multiply_fusion
  121.4 0.1 copy.37
  121.5 0.1 fusion.41
  121.7 0.6 fusion.69
  122.3 0.2 fusion.38
  122.5 0.4 convolution_bitcast_fusion.1
  122.8 0.4 fusion.31
  123.2 0.4 fusion.29
  123.7 0.4 convolution_bitcast_fusion.2
  124.1 0.8 pad_maximum_fusion
  124.9 0.3 convolution_bitcast_fusion.3
  125.4 10.2 %reduce-scatter.2.cloned.1.call-done = f32[192,128]{1,0:T(8,128)} async-done(((f32[384,128]{1,0:T(8,128)}), f32[192,128]{1,0:T(8,128)}) %reduce-scatter.2.cloned.1.call-update) | async-done | bytes 98320 | tf_op jit(solution)/shard_map/reduce_scatter | solution.py:380
  135.6 1.0 slice.133
  136.6 0.1 copy.44
  136.7 1.0 slice_bitcast_fusion.4
  137.7 0.1 slice_bitcast_fusion
  137.8 1.1 fusion.58
  138.8 0.1 copy.43
  138.9 13.0 %fusion.13 = (bf16[14848]{0:T(1024)(128)(2,1)S(1)}, f32[192]{0:T(256)S(1)}, f32[192]{0:T(256)S(1)}, bf16[14848]{0:T(1024)(128)(2,1)S(1)}, f32[192,14848]{1,0:T(8,128)}) fusion(bf16[192,14848]{1,0:T(8,128)(2,1)} %param.8, f32[192]{0:T(256)S(1)} %add_rsqrt_fusion, f32[192]{0:T(256)S(1)} %broadcast_multiply_fusion.2, f32[14848]{0:T(1024)S(1)} %get-tuple-element.16, ...), kind=kOutput, calls=%fused_computation.16 | convolution fusion | flops 2218641920 | bytes 28752896 | tf_op jit(solution)/shard_map/dot_general | solution.py:390
  152.0 4.7 %convolution_convert_fusion = bf16[14848,384]{1,0:T(8,128)(2,1)S(1)} fusion(bf16[1,14848]{1,0:T(2,128)(2,1)S(1)} %convert_element_type.96, bf16[1,14848]{1,0:T(2,128)(2,1)S(1)} %convert_element_type.94, bf16[192,14848]{1,0:T(8,128)(2,1)S(1)} %bitcast.103, bf16[208]{0:T(256)(128)(2,1)S(1)} %pad.15.clone, bf16[16,384]{0,1:T(8,128)(2,1)S(1)} %fusion.52, ...), kind=kOutput, calls=%fused_computation.1 | convolution fusion | flops 2402607104 | bytes 17324448 | tf_op jit(solution)/shard_map/dot_general | solution.py:403
  156.8 5.8 %copy.45 = bf16[2,4,2,2,464,384]{5,4,3,1,2,0:T(8,128)(2,1)} copy(bf16[2,4,2,2,464,384]{5,4,3,2,1,0:T(8,128)(2,1)S(1)} %bitcast.101) | data formatting | bytes 22806528 | tf_op jit(solution)/shard_map/reshape | solution.py:317
  162.5 86.8 %shard_map.112 = f32[464,384]{1,0:T(8,128)S(1)} custom-call(bf16[4,4,2,464,384]{4,3,2,1,0:T(8,128)(2,1)} %bitcast.100), custom_call_target="tpu_custom_call" | custom-call | tf_op jit(solution)/shard_map/pallas_call | solution.py:278
  249.4 0.9 slice_reduce_fusion
  250.3 1.1 copy.46
  251.4 10.3 %fusion.12 = bf16[192,14848]{1,0:T(8,128)(2,1)} fusion(bf16[192,14848]{1,0:T(8,128)(2,1)} %param.8, f32[192,14848]{1,0:T(8,128)} %get-tuple-element.35, f32[192]{0:T(256)S(1)} %get-tuple-element.36, f32[192]{0:T(256)S(1)} %get-tuple-element.37, f32[14848]{0:T(1024)S(1)} %get-tuple-element.16, f32[192]{0:T(256)S(1)} %add_rsqrt_fusion, ...), kind=kLoop, calls=%fused_computation.15 | loop fusion | flops 25657344 | bytes 22868992 | tf_op jit(solution)/shard_map/convert_element_type | solution.py:408
  (44 shorter events, 0.6 us)
Async XLA Ops:
  7.2 7.9 %copy-start.3 = (bf16[464]{0:T(512)(128)(2,1)S(1)}, bf16[464]{0:T(512)(128)(2,1)}, u32[]{:S(2)}) copy-start(bf16[464]{0:T(512)(128)(2,1)} %param.12) | copy-start | bytes 2788
  7.2 8.1 %copy-start.4 = (bf16[464]{0:T(512)(128)(2,1)S(1)}, bf16[464]{0:T(512)(128)(2,1)}, u32[]{:S(2)}) copy-start(bf16[464]{0:T(512)(128)(2,1)} %param.11) | copy-start | bytes 2788
  7.2 8.2 %copy-start.1 = (bf16[464,320]{0,1:T(8,128)(2,1)S(1)}, bf16[464,320]{0,1:T(8,128)(2,1)}, u32[]{:S(2)}) copy-start(bf16[464,320]{0,1:T(8,128)(2,1)} %param.10) | copy-start | bytes 890884
  7.2 128.4 %reduce-scatter.2.cloned.1.call-start = ((), (), s32[]{:S(2)}) async-start(), calls=%async_computation.1 | async-start | bytes 294912 | tf_op jit(solution)/shard_map/reduce_scatter | solution.py:380
  94.8 11.7 %copy-start = (bf16[2,2,4,2,464,384]{5,4,3,1,2,0:T(8,128)(2,1)}, bf16[2,2,4,2,464,384]{5,4,3,1,2,0:T(8,128)(2,1)S(1)}, u32[]{:S(2)}) copy-start(bf16[2,2,4,2,464,384]{5,4,3,1,2,0:T(8,128)(2,1)S(1)} %copy.32) | copy-start | bytes 34209796
  94.9 5.3 %slice-start = ((s8[5701632]{0:T(1024)(128)(4,1)}), s8[4194304]{0:T(1024)(128)(4,1)S(1)}, s32[]{:S(2)}) async-start(s8[5701632]{0:T(1024)(128)(4,1)} %bitcast.94), calls=%async_computation.2 | async-start | bytes 8388608
  94.9 6.8 %slice-start.1 = ((s8[5701632]{0:T(1024)(128)(4,1)}), s8[1507328]{0:T(1024)(128)(4,1)S(1)}, s32[]{:S(2)}) async-start(s8[5701632]{0:T(1024)(128)(4,1)} %bitcast.94), calls=%async_computation.3 | async-start | bytes 3014656
  106.5 14.2 %copy-start.2 = (bf16[192,192]{1,0:T(8,128)(2,1)S(1)}, bf16[192,192]{1,0:T(8,128)(2,1)}, u32[]{:S(2)}) copy-start(bf16[192,192]{1,0:T(8,128)(2,1)} %param.9) | copy-start | bytes 221188
  136.6 15.5 %slice-start.2 = ((s8[5701632]{0:T(1024)(128)(4,1)}), s8[1507328]{0:T(1024)(128)(4,1)S(1)}, s32[]{:S(2)}) async-start(s8[5701632]{0:T(1024)(128)(4,1)} %bitcast.102), calls=%async_computation.4 | async-start | bytes 3014656
  138.9 13.1 %slice-start.3 = ((s8[5701632]{0:T(1024)(128)(4,1)}), s8[4194304]{0:T(1024)(128)(4,1)S(1)}, s32[]{:S(2)}) async-start(s8[5701632]{0:T(1024)(128)(4,1)} %bitcast.102), calls=%async_computation.5 | async-start | bytes 8388608
Sparse Core Ops, SparseCore 0:
  125.0 10.5 reduce-scatter.1

commit v2 on v1

--- a/solution.py
+++ b/solution.py
@@ -63,98 +63,185 @@
     pl.semaphore_wait(barrier, Z + Q - 1)
 
 
-def gather_kernel(Z, L, own, out, local_sem, send_z, send_q, send_c, recv, recv_c):
+def gather_kernel(
+    Z, L, own, hidden, out, centre, variance, held,
+    local_sem, send_z, send_x, send_y, send_r0, send_r1, send_c,
+    recv, recv_0, recv_1, recv_c,
+):
     Q = 2 * L
+    rows = own.shape[0]
+    half = -(-(rows // 2) // 16) * 16
     z, q, c = place(Z, L)
+    l, x = q // 2, q % 2
     greet(Z, Q, z, q, c)
 
-    def remote(src, zz, qq, send, got, target):
+    def block(zz, qq):
+        return out.at[qq // 2, zz, qq % 2, c]
+
+    def remote(src, dst, send, got, target):
         return pltpu.make_async_remote_copy(
-            src_ref=src,
-            dst_ref=out.at[qq, zz, c],
-            send_sem=send,
-            recv_sem=got,
-            device_id=target,
-            device_id_type=MESH,
-        )
-
-    mine = pltpu.make_async_copy(own, out.at[q, z, c], local_sem)
+            src_ref=src, dst_ref=dst, send_sem=send, recv_sem=got,
+            device_id=target, device_id_type=MESH,
+        )
+
+    across = q + 1 - 2 * x
+
+    def beside(d):
+        return ((l + d) % L) * 2 + x
+
+    mine = pltpu.make_async_copy(own, block(z, q), local_sem.at[0])
     mine.start()
+    fetch = pltpu.make_async_copy(hidden, held, local_sem.at[1])
+    fetch.start()
 
     def to_z(d):
-        return remote(own, z, q, send_z.at[d - 1], recv.at[q, z], device((z + d) % Z, q, c))
-
-    def to_q(k, d, src):
-        zz = (z + Z - k) % Z
-        return remote(src, zz, q, send_q.at[k, d - 1], recv.at[q, zz], device(z, (q + d) % Q, c))
+        return remote(
+            own, block(z, q), send_z.at[d - 1], recv.at[q, z], device((z + d) % Z, q, c)
+        )
+
+    def to_x(zz, src):
+        return remote(src, block(zz, q), send_x.at[zz], recv.at[q, zz], device(z, across, c))
+
+    def to_y(zz, d, src):
+        return remote(
+            src, block(zz, q), send_y.at[zz, d - 1], recv.at[q, zz], device(z, beside(d), c)
+        )
+
+    def relay_x(zz, d):
+        part = block(zz, beside(d)).at[pl.ds(0, half)]
+        return remote(
+            part, part, send_r0.at[zz, d - 1], recv_0.at[beside(d), zz], device(z, across, c)
+        )
+
+    def relay_y(zz, d):
+        part = block(zz, across).at[pl.ds(half, rows - half)]
+        return remote(
+            part, part, send_r1.at[zz, d - 1], recv_1.at[across, zz], device(z, beside(d), c)
+        )
 
     def to_c(zz, qq, src):
-        return remote(src, zz, qq, send_c.at[qq, zz], recv_c.at[qq, zz], device(z, q, 1 - c))
+        return remote(src, block(zz, qq), send_c.at[qq, zz], recv_c.at[qq, zz], device(z, q, 1 - c))
 
     def landed(zz, qq):
-        pltpu.make_async_copy(own, out.at[qq, zz, c], recv.at[qq, zz]).wait()
+        pltpu.make_async_copy(own, block(zz, qq), recv.at[qq, zz]).wait()
 
     for d in range(1, Z):
         to_z(d).start()
-    for d in range(1, Q):
-        to_q(0, d, own).start()
+    to_x(z, own).start()
+    for d in range(1, L):
+        to_y(z, d, own).start()
     to_c(z, q, own).start()
 
-    def spread(k, carry):
+    fetch.wait()
+    width = held.shape[1]
+
+    def stats(g, carry):
+        span = pl.ds(pl.multiple_of(g * 16, 16), 16)
+        mean = jnp.sum(held[span, :].astype(jnp.float32), axis=1, keepdims=True) / width
+        shifted = held[span, :].astype(jnp.float32) - mean
+        spread_of = jnp.sum(shifted * shifted, axis=1, keepdims=True) / width
+        centre[span, :] = jnp.broadcast_to(mean, (16, 128))
+        variance[span, :] = jnp.broadcast_to(spread_of, (16, 128))
+        return carry
+
+    lax.fori_loop(0, held.shape[0] // 16, stats, 0)
+
+    def spread(k):
         zz = (z + Z - k) % Z
         landed(zz, q)
-        for d in range(1, Q):
-            to_q(k, d, out.at[q, zz, c]).start()
-        to_c(zz, q, out.at[q, zz, c]).start()
-        return carry
-
-    lax.fori_loop(1, Z, spread, 0)
-
-    def forward(k, carry):
+        to_x(zz, block(zz, q)).start()
+        for d in range(1, L):
+            to_y(zz, d, block(zz, q)).start()
+        to_c(zz, q, block(zz, q)).start()
+
+    def relay(k):
         zz = (z + Z - k) % Z
-        for d in range(1, Q):
-            qq = (q + d) % Q
-            landed(zz, qq)
-            to_c(zz, qq, out.at[qq, zz, c]).start()
-        return carry
-
-    lax.fori_loop(0, Z, forward, 0)
+        landed(zz, across)
+        for d in range(1, L):
+            relay_y(zz, d).start()
+        to_c(zz, across, block(zz, across)).start()
+        for d in range(1, L):
+            landed(zz, beside(d))
+            relay_x(zz, d).start()
+            to_c(zz, beside(d), block(zz, beside(d))).start()
+
+    def middle(k, carry):
+        spread(k)
+        relay(k - 1)
+        return carry
+
+    lax.fori_loop(1, Z, middle, 0)
+    relay(Z - 1)
+
+    def corners(k, carry):
+        zz = (z + Z - k) % Z
+        for d in range(1, L):
+            qq = beside(d) + 1 - 2 * x
+            at = block(zz, qq)
+            low, high = pl.ds(0, half), pl.ds(half, rows - half)
+            pltpu.make_async_copy(own.at[low], at.at[low], recv_0.at[qq, zz]).wait()
+            pltpu.make_async_copy(own.at[high], at.at[high], recv_1.at[qq, zz]).wait()
+            to_c(zz, qq, at).start()
+        return carry
+
+    lax.fori_loop(0, Z, corners, 0)
 
     mine.wait()
     for d in range(1, Z):
         to_z(d).wait_send()
 
     def finish(k, carry):
-        for d in range(1, Q):
-            to_q(k, d, own).wait_send()
+        to_x(k, own).wait_send()
+        for d in range(1, L):
+            to_y(k, d, own).wait_send()
+            relay_x(k, d).wait_send()
+            relay_y(k, d).wait_send()
         for d in range(Q):
-            to_c(k, (q + d) % Q, own).wait_send()
-            pltpu.make_async_copy(
-                own, out.at[(q + d) % Q, k, 1 - c], recv_c.at[(q + d) % Q, k]
-            ).wait()
+            qq = (q + d) % Q
+            to_c(k, qq, own).wait_send()
+            pltpu.make_async_copy(own, out.at[qq // 2, k, qq % 2, 1 - c], recv_c.at[qq, k]).wait()
         return carry
 
     lax.fori_loop(0, Z, finish, 0)
 
 
-def gather(block, Z, L):
+def gather(block, hidden, Z, L):
     rows = block.shape[0]
+    tokens = hidden.shape[0]
     Q = 2 * L
+    dma = pltpu.SemaphoreType.DMA
+    others = max(L - 1, 1)
     return pl.pallas_call(
         functools.partial(gather_kernel, Z, L),
-        out_shape=jax.ShapeDtypeStruct((Q, Z, 2, rows, LANES), jnp.bfloat16),
-        in_specs=[pl.BlockSpec(memory_space=pl.ANY)],
-        out_specs=pl.BlockSpec(memory_space=pl.ANY),
+        out_shape=(
+            jax.ShapeDtypeStruct((L, Z, 2, 2, rows, LANES), jnp.bfloat16),
+            jax.ShapeDtypeStruct((tokens, 128), jnp.float32),
+            jax.ShapeDtypeStruct((tokens, 128), jnp.float32),
+        ),
+        in_specs=[pl.BlockSpec(memory_space=pl.ANY)] * 2,
+        out_specs=(
+            pl.BlockSpec(memory_space=pl.ANY),
+            pl.BlockSpec(memory_space=pltpu.VMEM),
+            pl.BlockSpec(memory_space=pltpu.VMEM),
+        ),
         scratch_shapes=[
-            pltpu.SemaphoreType.DMA,
-            pltpu.SemaphoreType.DMA((max(Z - 1, 1),)),
-            pltpu.SemaphoreType.DMA((Z, Q - 1)),
-            pltpu.SemaphoreType.DMA((Q, Z)),
-            pltpu.SemaphoreType.DMA((Q, Z)),
-            pltpu.SemaphoreType.DMA((Q, Z)),
+            pltpu.VMEM(hidden.shape, jnp.bfloat16),
+            dma((2,)),
+            dma((max(Z - 1, 1),)),
+            dma((Z,)),
+            dma((Z, others)),
+            dma((Z, others)),
+            dma((Z, others)),
+            dma((Q, Z)),
+            dma((Q, Z)),
+            dma((Q, Z)),
+            dma((Q, Z)),
+            dma((Q, Z)),
         ],
-        compiler_params=pltpu.CompilerParams(collective_id=0, has_side_effects=True),
-    )(block)
+        compiler_params=pltpu.CompilerParams(
+            collective_id=0, has_side_effects=True, vmem_limit_bytes=32 * 2**20
+        ),
+    )(block, hidden)
 
 
 def scatter_kernel(
@@ -166,11 +253,11 @@
     greet(Z, Q, z, q, c)
 
     def load(zz, qq):
-        return pltpu.make_async_copy(part.at[qq, zz, c], own.at[qq, zz], sem_own.at[qq, zz])
+        return pltpu.make_async_copy(part.at[qq // 2, zz, qq % 2, c], own.at[qq, zz], sem_own.at[qq, zz])
 
     def to_c(zz, qq):
         return pltpu.make_async_remote_copy(
-            src_ref=part.at[qq, zz, 1 - c],
+            src_ref=part.at[qq // 2, zz, qq % 2, 1 - c],
             dst_ref=pair.at[qq, zz],
             send_sem=send_c.at[qq, zz],
             recv_sem=recv_c.at[qq, zz],
@@ -214,7 +301,7 @@
         total = own[qq, zz].astype(jnp.float32) + pair[qq, zz].astype(jnp.float32)
         own[qq, zz] = total.astype(jnp.bfloat16)
 
-    def pairs(k, carry):
+    def pairs(k):
         zz = (z + k) % Z
 
         def one(d, carry):
@@ -225,9 +312,8 @@
 
         lax.fori_loop(1, Q, one, 0)
         join(zz, q)
-        return carry
-
-    lax.fori_loop(1, Z + 1, pairs, 0)
+
+    pairs(1)
 
     def plane_sum(zz):
         tall[zz] = own[q, zz].astype(jnp.float32)
@@ -241,6 +327,7 @@
         lax.fori_loop(1, Q, add, 0)
 
     def columns(k, carry):
+        pairs(k + 1)
         zz = (z + k) % Z
         plane_sum(zz)
         to_z(zz).start()
@@ -309,29 +396,24 @@
     query_cols = QH * HD
 
     def whole(blocks):
-        blocks = blocks[:, :, :, :shard]
-        blocks = blocks.reshape((L, 2, Z, 2) + blocks.shape[3:])
-        return blocks.transpose(0, 2, 1, 3, 4, 5).reshape(model_width, -1)
+        return blocks[..., :shard, :].reshape(model_width, LANES)
 
     def apart(rows):
-        blocks = rows.reshape(L, Z, 2, 2, shard, -1).transpose(0, 2, 1, 3, 4, 5)
-        blocks = blocks.reshape(2 * L, Z, 2, shard, -1)
-        return jnp.pad(blocks, ((0, 0), (0, 0), (0, 0), (0, padded - shard), (0, 0)))
+        blocks = rows.reshape(L, Z, 2, 2, shard, LANES)
+        return jnp.pad(blocks, ((0, 0),) * 4 + ((0, padded - shard), (0, 0)))
 
     own_block = jnp.concatenate([w_qkv, ln_gain[:, None], ln_bias[:, None]], axis=1)
     own_block = jnp.pad(own_block, ((0, padded - shard), (0, LANES - qkv - 2)))
-    w_all = whole(gather(own_block, Z, L))
+    blocks, centre, variance = gather(own_block, hidden_in, Z, L)
+    w_all = whole(blocks)
     picks = jnp.arange(16)[:, None] + qkv == jnp.arange(LANES)[None, :]
     picks = (picks & (jnp.arange(16) < 2)[:, None]).astype(jnp.bfloat16)
     contract = (((1,), (1,)), ((), ()))
     rows = lax.dot_general(picks, w_all, contract, preferred_element_type=jnp.float32)
     gain, bias = rows[0:1], rows[1:2]
     values = hidden_in.astype(jnp.float32)
-    centre = jnp.mean(values, axis=-1, keepdims=True)
-    shifted = values - centre
-    variance = jnp.mean(shifted * shifted, axis=-1, keepdims=True)
-    inverse = lax.rsqrt(variance + epsilon)
-    normalized = shifted * inverse
+    inverse = lax.rsqrt(variance[:, :1] + epsilon)
+    normalized = (values - centre[:, :1]) * inverse
     normed = (normalized * gain + bias).astype(jnp.bfloat16)
     proj_total = jnp.dot(normed, w_all, preferred_element_type=jnp.float32)[:, :qkv]
     positions = lax.axis_index("local") * tok_rows + jnp.arange(tok_rows, dtype=jnp.int32)
@@ -345,7 +427,10 @@
     pair_own = jnp.concatenate([keys_own, proj_total[:, query_cols + HD :]], axis=1).astype(
         jnp.bfloat16
     )
-    pair_all = lax.all_gather(pair_own, "local", axis=0, tiled=True)
+    def shifted_by(array, d):
+        return lax.ppermute(array, "local", [(s, (s + d) % L) for s in range(L)])
+
+    pair_all = jnp.concatenate([pair_own] + [shifted_by(pair_own, L - d) for d in range(1, L)])
     seq_rows = pair_all.shape[0]
     keys_all = pair_all[:, :HD]
     values_all = pair_all[:, HD:]
@@ -353,7 +438,9 @@
     weight = lax.dynamic_slice(priority, (sample_index[0],), (1,))[0]
     scale = HD ** (-0.5)
     scores = jnp.einsum("qhd,kd->hqk", query, keys_all, preferred_element_type=jnp.float32) * scale
-    key_positions = jnp.arange(seq_rows, dtype=jnp.int32)
+    key_positions = (
+        lax.axis_index("local") * tok_rows + jnp.arange(seq_rows, dtype=jnp.int32)
+    ) % seq_rows
     allowed = (key_positions[None, :] <= positions[:, None]) & (key_positions[None, :] < length)
     scores = jnp.where(allowed[None], scores, -1e30)
     row_max = jnp.max(scores, axis=-1, keepdims=True)
@@ -377,12 +464,10 @@
     d_value_term = jnp.einsum(
         "hqk,qhd->kd", attention_b, cotangent, preferred_element_type=jnp.float32
     )
-    d_pair = lax.psum_scatter(
-        jnp.concatenate([d_key_term, d_value_term], axis=1),
-        "local",
-        scatter_dimension=0,
-        tiled=True,
-    )
+    d_pair_term = jnp.concatenate([d_key_term, d_value_term], axis=1)
+    d_pair = d_pair_term[:tok_rows]
+    for d in range(1, L):
+        d_pair += shifted_by(d_pair_term[d * tok_rows : (d + 1) * tok_rows], d)
     d_query_pre = unrotate(d_query, cosine, sine_table).reshape(tok_rows, query_cols)
     d_key_pre = unrotate(d_pair[:, None, :HD], cosine, sine_table)[:, 0, :]
     d_projected = jnp.concatenate([d_query_pre, d_key_pre, d_pair[:, HD:]], axis=1)

time: 269 us -> 230 us (0.86)
  between operations: 15.8 us -> 2.4 us
  other arithmetic: 27.8 us -> 18 us
  local copies, waits for them, and re-layouts: 22.5 us -> 14.1 us
  matrix products: 28.5 us -> 35.7 us
  Pallas kernels: 159 us -> 152 us
  waiting for transfers between devices: 10.2 us -> 4.68 us
  blocking collectives: 4.96 us -> 0 us
    reshape x2 -> x0, local copies, waits for them, and re-layouts: 12.2 us -> none  [the longest x1 6.43 us: whole(): blocks = blocks.reshape((L, 2, Z, 2) + blocks.shape[3:])]
    pallas_call x1, Pallas kernels: 71.9 us -> 60.5 us  [gather(): pl.pallas_call(functools.partial(gather_kernel, Z, L), out_shape=(jax.Sha...]
    reduce_scatter x1 -> x0, waiting for transfers between devices: 10.2 us -> none  [on_device(): lax.psum_scatter(jnp.concatenate([d_key_term, d_value_term], axis=1), 'lo...]
    reduce_sum x2 -> x0, other arithmetic: 7.8 us -> none  [the longest x1 4.27 us: on_device(): variance = jnp.mean(shifted * shifted, axis=-1, keepdims=True)]
    pallas_call x1, Pallas kernels: 86.8 us -> 91.9 us  [scatter_sum(): pl.pallas_call(functools.partial(scatter_kernel, Z, L), out_shape=jax.Sha...]
    all_gather x1 -> x0, blocking collectives: 4.96 us -> none  [on_device(): pair_all = lax.all_gather(pair_own, 'local', axis=0, tiled=True)]
    ppermute x0 -> x2, waiting for transfers between devices: none -> 4.68 us  [shifted_by(): return lax.ppermute(array, 'local', [(s, (s + d) % L) for s in range(L)])]
    dot_general x1, matrix products: 3.05 us -> 7.44 us  [on_device(): lax.dot_general(picks, w_all, contract, preferred_element_type=jnp.float32)]
  transfers between devices with their start and end apart: 1 -> 2, of which waited for: 1 -> 1; matrix products, arithmetic and copies ran while one was open for 0% -> 1% of each run, Pallas kernels for 0% -> 0%
where the time goes in v2:
time: 230 us
  Pallas kernels  152 us (66%)
  matrix products  35.7 us (16%)
  other arithmetic  18 us (8%)
  local copies, waits for them, and re-layouts  14.1 us (6%)
  waiting for transfers between devices  4.68 us (2%)
  between operations  2.4 us (1%)
    pallas_call x1, Pallas kernels, scatter_sum(): pl.pallas_call(functools.partial(scatter_kernel, Z, L), out_shape=jax.Sha...  91.9 us
    pallas_call x1, Pallas kernels, gather(): pl.pallas_call(functools.partial(gather_kernel, Z, L), out_shape=(jax.Sha...  60.5 us
    dot_general x1, matrix products, on_device(): lax.dot_general(d_projected, w_all, contract, preferred_element_type=jnp....  13.3 us
    convert_element_type x1, other arithmetic, on_device(): grad_input.astype(jnp.bfloat16)  10.3 us
    unnamed x18, local copies, waits for them, and re-layouts  9.1 us
    dot_general x1, matrix products, on_device(): lax.dot_general(picks, w_all, contract, preferred_element_type=jnp.float32)  7.44 us
    dot_general x1, matrix products, on_device(): lax.dot_general(left, right, (((0,), (0,)), ((), ())), preferred_element_...  7.17 us
    dot_general x1, matrix products, on_device(): jnp.dot(normed, w_all, preferred_element_type=jnp.float32)[:, :qkv]  5.32 us
  transfers between devices with their start and end apart: 2, of which 1 were waited for; matrix products, arithmetic and copies ran while one was open for 1% of the time, Pallas kernels for 0%

profile of v2, /device:TPU:0, one launch (start us, length us, event | category | flops | bytes accessed | tf_op | source)
XLA Modules:
  0.0 229.5 jit_solution(4333660047967748355)
XLA Ops:
  0.7 0.8 broadcast_in_dim.30
  1.5 0.8 broadcast_in_dim.29
  2.3 1.2 copy.28
  3.5 0.1 fusion.26.own
  3.7 2.6 %copy-done = bf16[192,14848]{1,0:T(8,128)(2,1)S(1)} copy-done((bf16[192,14848]{1,0:T(8,128)(2,1)S(1)}, bf16[192,14848]{1,0:T(8,128)(2,1)}, u32[]{:S(2)}) %copy-start) | copy-done | bytes 5701656
  6.3 60.5 %shard_map.111 = (bf16[2,4,2,2,464,384]{5,4,3,2,1,0:T(8,128)(2,1)S(1)}, f32[192,128]{1,0:T(8,128)S(1)}, f32[192,128]{1,0:T(8,128)S(1)}) custom-call(bf16[464,384]{1,0:T(8,128)(2,1)S(1)} %fusion.26.own, bf16[192,14848]{1,0:T(8,128)(2,1)S(1)} %copy-done), custom_call_target="tpu_custom_call" | custom-call | tf_op jit(solution)/shard_map/pallas_call | solution.py:214
  66.8 4.2 %copy-done.1 = bf16[2,4,2,2,464,384]{5,4,3,2,1,0:T(8,128)(2,1)} copy-done((bf16[2,4,2,2,464,384]{5,4,3,2,1,0:T(8,128)(2,1)}, bf16[2,4,2,2,464,384]{5,4,3,2,1,0:T(8,128)(2,1)S(1)}, u32[]{:S(2)}) %copy-start.1) | copy-done | bytes 11403288
  71.0 7.4 %fusion.47 = f32[16,14848]{1,0:T(8,128)S(1)} fusion(bf16[14848,384]{1,0:T(8,128)(2,1)} %bitcast.89, s32[16]{0:T(128)S(1)} %iota_add_fusion.1, pred[16]{0:T(512)(128)(4,1)S(1)} %iota_compare_fusion.3), kind=kOutput, calls=%fused_computation.98 | convolution fusion | flops 182470656 | bytes 12353616 | tf_op jit(solution)/shard_map/dot_general | solution.py:412
  78.4 0.3 slice_reduce_fusion.4
  78.7 0.1 slice_reduce_fusion.2
  78.9 4.9 %add_convert_fusion = bf16[192,14848]{1,0:T(8,128)(2,1)} fusion(bf16[192,14848]{1,0:T(8,128)(2,1)S(1)} %bitcast.88, f32[14848]{0:T(1024)S(1)} %get-tuple-element.23, f32[14848]{0:T(1024)S(1)} %get-tuple-element.22, f32[192]{0:T(256)S(1)} %get-tuple-element.42, f32[192]{0:T(256)S(1)} %get-tuple-element.43), kind=kLoop, calls=%fused_computation.5 | loop fusion | flops 17104896 | bytes 11523584 | tf_op jit(solution)/shard_map/convert_element_type | solution.py:417
  83.8 5.3 %fusion.60 = f32[192,384]{1,0:T(8,128)S(1)} fusion(bf16[192,14848]{1,0:T(8,128)(2,1)} %add_convert_fusion, bf16[14848,384]{1,0:T(8,128)(2,1)S(1)} %bitcast.91), kind=kOutput, calls=%fused_computation.119 | convolution fusion | flops 2189426688 | bytes 17399808 | tf_op jit(solution)/shard_map/dot_general | solution.py:418
  89.2 0.1 slice_bitcast_fusion.5
  89.3 0.1 fusion.41
  89.4 0.4 multiply_cosine_fusion
  89.8 0.2 fusion.43
  90.0 0.1 pad_maximum_fusion.4
  90.1 2.2 collective-permute-start
  92.3 0.1 copy.31
  92.5 0.1 copy.33
  92.6 0.1 copy.32
  94.0 1.3 dynamic_slice.3
  95.3 0.7 convert_multiply_fusion
  95.9 0.1 copy.35
  96.1 0.1 compare_and_fusion
  96.3 0.1 pad_maximum_fusion.3
  96.4 0.6 fusion.59
  97.0 0.2 fusion.24
  97.2 0.4 convolution_bitcast_fusion.1
  97.6 0.4 fusion.17
  98.0 0.4 fusion.15
  98.4 0.4 convolution_bitcast_fusion.2
  98.8 0.3 convolution_bitcast_fusion.3
  99.1 0.1 pad_maximum_fusion
  99.2 0.1 collective-permute-start.1
  99.3 4.7 %collective-permute-done.1 = f32[192,128]{1,0:T(8,128)S(1)} collective-permute-done((f32[192,128]{1,0:T(8,128)S(1)}, f32[192,128]{1,0:T(8,128)S(1)}, u32[]{:S(2)}, u32[]{:S(2)}) %collective-permute-start.1) | collective-permute-done | bytes 98336 | tf_op jit(solution)/shard_map/ppermute | solution.py:431
  104.0 0.1 fusion.39
  104.1 0.1 slice.161
  104.2 0.1 copy.42
  104.3 0.1 slice_bitcast_fusion
  104.4 0.2 fusion.45
  104.6 0.1 copy.41
  104.7 13.3 %multiply_reduce_fusion = (bf16[14848]{0:T(1024)(128)(2,1)S(1)}, f32[192]{0:T(256)S(1)}, f32[192]{0:T(256)S(1)}, bf16[14848]{0:T(1024)(128)(2,1)S(1)}, f32[192,14848]{1,0:T(8,128)}) fusion(bf16[192,14848]{1,0:T(8,128)(2,1)} %hidden.1, f32[192]{0:T(256)S(1)} %get-tuple-element.42, f32[192]{0:T(256)S(1)} %get-tuple-element.43, ...), kind=kOutput, calls=%fused_computation.2 | convolution fusion | flops 2218641920 | bytes 28752896 | tf_op jit(solution)/shard_map/dot_general | solution.py:475
  118.2 7.2 %convolution_convert_fusion = bf16[14848,384]{1,0:T(8,128)(2,1)} fusion(bf16[1,14848]{1,0:T(2,128)(2,1)S(1)} %convert_element_type.96, bf16[1,14848]{1,0:T(2,128)(2,1)S(1)} %convert_element_type.94, bf16[192,14848]{1,0:T(8,128)(2,1)S(1)} %bitcast.95, bf16[208]{0:T(256)(128)(2,1)S(1)} %pad.15.clone, bf16[16,384]{0,1:T(8,128)(2,1)S(1)} %fusion.37, ...), kind=kOutput, calls=%fused_computation.1 | convolution fusion | flops 2402607104 | bytes 17324448 | tf_op jit(solution)/shard_map/dot_general | solution.py:488
  125.3 91.9 %shard_map.112 = f32[464,384]{1,0:T(8,128)S(1)} custom-call(bf16[2,4,2,2,464,384]{5,4,3,2,1,0:T(8,128)(2,1)} %bitcast.93), custom_call_target="tpu_custom_call" | custom-call | tf_op jit(solution)/shard_map/pallas_call | solution.py:365
  217.2 0.9 slice_reduce_fusion
  218.2 1.1 copy.43
  219.3 10.3 %multiply_convert_fusion = bf16[192,14848]{1,0:T(8,128)(2,1)} fusion(bf16[192,14848]{1,0:T(8,128)(2,1)} %hidden.1, f32[192,14848]{1,0:T(8,128)} %get-tuple-element.41, f32[192]{0:T(256)S(1)} %broadcast_multiply_fusion, f32[192]{0:T(256)S(1)} %broadcast_multiply_fusion.1, f32[14848]{0:T(1024)S(1)} %get-tuple-element.22, f32[192]{0:T(256)S(1)} %get-tuple-element.42, ...), kind=kLoop, calls=%fused_computation.3 | loop fusion | flops 25657344 | bytes 22868992 | tf_op jit(solution)/shard_map/convert_element_type | solution.py:493
  (41 shorter events, 0.5 us)
Async XLA Ops:
  3.7 2.6 %copy-start = (bf16[192,14848]{1,0:T(8,128)(2,1)S(1)}, bf16[192,14848]{1,0:T(8,128)(2,1)}, u32[]{:S(2)}) copy-start(bf16[192,14848]{1,0:T(8,128)(2,1)} %hidden.1) | copy-start | bytes 17104900
  6.3 72.6 %slice-start = ((s8[5701632]{0:T(1024)(128)(4,1)}), s8[1507328]{0:T(1024)(128)(4,1)S(1)}, s32[]{:S(2)}) async-start(s8[5701632]{0:T(1024)(128)(4,1)} %bitcast.87), calls=%async_computation | async-start | bytes 3014656
  66.8 4.2 %copy-start.1 = (bf16[2,4,2,2,464,384]{5,4,3,2,1,0:T(8,128)(2,1)}, bf16[2,4,2,2,464,384]{5,4,3,2,1,0:T(8,128)(2,1)S(1)}, u32[]{:S(2)}) copy-start(bf16[2,4,2,2,464,384]{5,4,3,2,1,0:T(8,128)(2,1)S(1)} %get-tuple-element.9) | copy-start | bytes 34209796
  71.0 7.9 %slice-start.1 = ((s8[5701632]{0:T(1024)(128)(4,1)}), s8[4194304]{0:T(1024)(128)(4,1)S(1)}, s32[]{:S(2)}) async-start(s8[5701632]{0:T(1024)(128)(4,1)} %bitcast.87), calls=%async_computation.1 | async-start | bytes 8388608
  71.0 12.9 %copy-start.2 = (bf16[2,4,2,2,464,384]{5,4,3,2,1,0:T(8,128)(2,1)S(1)}, bf16[2,4,2,2,464,384]{5,4,3,2,1,0:T(8,128)(2,1)}, u32[]{:S(2)}) copy-start(bf16[2,4,2,2,464,384]{5,4,3,2,1,0:T(8,128)(2,1)} %copy-done.1) | copy-start | bytes 34209796
  83.8 11.4 %copy-start.3 = (bf16[192,192]{1,0:T(8,128)(2,1)S(1)}, bf16[192,192]{1,0:T(8,128)(2,1)}, u32[]{:S(2)}) copy-start(bf16[192,192]{1,0:T(8,128)(2,1)} %param.9) | copy-start | bytes 221188
  90.1 6.3 %collective-permute-start = (bf16[192,128]{1,0:T(8,128)(2,1)S(1)}, bf16[192,128]{1,0:T(8,128)(2,1)S(1)}, u32[]{:S(2)}, u32[]{:S(2)}) collective-permute-start(bf16[192,128]{1,0:T(8,128)(2,1)S(1)} %pad_maximum_fusion.4), channel_id=1, source_target_pairs={{0,1},{1,0},{2,3},{3,2},{4,5},{5,4},{6,7},{7,6},{8,9},{9,8},{10,11... | collective-permute-start | bytes 147464 | tf_op jit(solution)/shard_map/ppermute | solution.py:431
  99.2 4.8 %collective-permute-start.1 = (f32[192,128]{1,0:T(8,128)S(1)}, f32[192,128]{1,0:T(8,128)S(1)}, u32[]{:S(2)}, u32[]{:S(2)}) collective-permute-start(f32[192,128]{1,0:T(8,128)S(1)} %pad_maximum_fusion), channel_id=1, source_target_pairs={{0,1},{1,0},{2,3},{3,2},{4,5},{5,4},{6,7},{7,6},{8,9},{9,8},{10,11... | collective-permute-start | bytes 294920 | tf_op jit(solution)/shard_map/ppermute | solution.py:431
  104.1 14.0 %slice-start.2 = ((s8[5701632]{0:T(1024)(128)(4,1)}), s8[1507328]{0:T(1024)(128)(4,1)S(1)}, s32[]{:S(2)}) async-start(s8[5701632]{0:T(1024)(128)(4,1)} %bitcast.94), calls=%async_computation.2 | async-start | bytes 3014656
  104.7 13.5 %slice-start.3 = ((s8[5701632]{0:T(1024)(128)(4,1)}), s8[4194304]{0:T(1024)(128)(4,1)S(1)}, s32[]{:S(2)}) async-start(s8[5701632]{0:T(1024)(128)(4,1)} %bitcast.94), calls=%async_computation.3 | async-start | bytes 8388608

commit v3 on v2

--- a/solution.py
+++ b/solution.py
@@ -245,10 +245,12 @@
 
 
 def scatter_kernel(
-    Z, L, part, out, own, pair, plane, tall, column,
-    sem_own, send_c, recv_c, send_q, recv_q, send_z, recv_z,
+    Z, L, part, vectors, out, own, pair, pair_vectors, packed, plane, tall, column,
+    sem_own, sem_vectors, send_c, recv_c, send_q, recv_q, send_z, recv_z,
 ):
     Q = 2 * L
+    rows = own.shape[2]
+    half = rows // 2
     z, q, c = place(Z, L)
     greet(Z, Q, z, q, c)
 
@@ -267,7 +269,7 @@
 
     def to_q(zz, qq):
         return pltpu.make_async_remote_copy(
-            src_ref=own.at[qq, zz],
+            src_ref=packed.at[qq, zz],
             dst_ref=plane.at[zz, q],
             send_sem=send_q.at[qq, zz],
             recv_sem=recv_q.at[zz, q],
@@ -285,6 +287,16 @@
             device_id_type=MESH,
         )
 
+    other_vectors = pltpu.make_async_remote_copy(
+        src_ref=vectors.at[1 - c],
+        dst_ref=pair_vectors,
+        send_sem=sem_vectors.at[0],
+        recv_sem=sem_vectors.at[1],
+        device_id=device(z, q, 1 - c),
+        device_id_type=MESH,
+    )
+    other_vectors.start()
+
     def begin(k, carry):
         zz = (z + k) % Z
         for d in range(Q):
@@ -298,8 +310,16 @@
     def join(zz, qq):
         load(zz, qq).wait()
         to_c(zz, qq).wait_recv()
-        total = own[qq, zz].astype(jnp.float32) + pair[qq, zz].astype(jnp.float32)
-        own[qq, zz] = total.astype(jnp.bfloat16)
+        def total(r, n, lane):
+            at = (qq, zz, slice(r, r + n), slice(lane, lane + 128))
+            return own[at].astype(jnp.float32) + pair[at].astype(jnp.float32)
+
+        packed[qq, zz, 0:rows] = total(0, rows, 0).astype(jnp.bfloat16)
+        packed[qq, zz, rows : 2 * rows] = total(0, rows, 128).astype(jnp.bfloat16)
+        tail = total(0, rows, 256)
+        tail = tail[:half] + pltpu.roll(tail[half:], 64, 1)
+        ends = vectors[c, qq, zz] + pair_vectors[qq, zz]
+        packed[qq, zz, 2 * rows :] = jnp.concatenate([tail, ends], axis=0).astype(jnp.bfloat16)
 
     def pairs(k):
         zz = (z + k) % Z
@@ -313,14 +333,15 @@
         lax.fori_loop(1, Q, one, 0)
         join(zz, q)
 
+    other_vectors.wait()
     pairs(1)
 
     def plane_sum(zz):
-        tall[zz] = own[q, zz].astype(jnp.float32)
+        tall[zz] = packed[q, zz].astype(jnp.float32)
 
         def add(d, carry):
             qq = (q + d) % Q
-            pltpu.make_async_copy(own.at[qq, zz], plane.at[zz, qq], recv_q.at[zz, qq]).wait()
+            pltpu.make_async_copy(packed.at[qq, zz], plane.at[zz, qq], recv_q.at[zz, qq]).wait()
             tall[zz] += plane[zz, qq].astype(jnp.float32)
             return carry
 
@@ -358,22 +379,27 @@
         to_z((z + d) % Z).wait_send()
 
 
-def scatter_sum(part, Z, L):
+def scatter_sum(part, vectors, Z, L):
     rows = part.shape[-2]
+    ends = vectors.shape[-2]
+    tall = 2 * rows + rows // 2 + ends
     Q = 2 * L
     dma = pltpu.SemaphoreType.DMA
     return pl.pallas_call(
         functools.partial(scatter_kernel, Z, L),
-        out_shape=jax.ShapeDtypeStruct((rows, LANES), jnp.float32),
-        in_specs=[pl.BlockSpec(memory_space=pl.ANY)],
+        out_shape=jax.ShapeDtypeStruct((tall, 128), jnp.float32),
+        in_specs=[pl.BlockSpec(memory_space=pl.ANY), pl.BlockSpec(memory_space=pltpu.VMEM)],
         out_specs=pl.BlockSpec(memory_space=pltpu.VMEM),
         scratch_shapes=[
             pltpu.VMEM((Q, Z, rows, LANES), jnp.bfloat16),
             pltpu.VMEM((Q, Z, rows, LANES), jnp.bfloat16),
-            pltpu.VMEM((Z, Q, rows, LANES), jnp.bfloat16),
-            pltpu.VMEM((Z, rows, LANES), jnp.float32),
-            pltpu.VMEM((Z, rows, LANES), jnp.float32),
-            dma((Q, Z)),
+            pltpu.VMEM((Q, Z, ends, 128), jnp.float32),
+            pltpu.VMEM((Q, Z, tall, 128), jnp.bfloat16),
+            pltpu.VMEM((Z, Q, tall, 128), jnp.bfloat16),
+            pltpu.VMEM((Z, tall, 128), jnp.float32),
+            pltpu.VMEM((Z, tall, 128), jnp.float32),
+            dma((Q, Z)),
+            dma((2,)),
             dma((Q, Z)),
             dma((Q, Z)),
             dma((Q, Z)),
@@ -384,7 +410,7 @@
         compiler_params=pltpu.CompilerParams(
             collective_id=1, has_side_effects=True, vmem_limit_bytes=44 * 2**20
         ),
-    )(part)
+    )(part, vectors)
 
 
 def on_device(
@@ -481,19 +507,25 @@
     )
     term_gain = jnp.sum(d_normed * normalized, axis=0, keepdims=True).astype(jnp.bfloat16)
     term_bias = jnp.sum(d_normed, axis=0, keepdims=True).astype(jnp.bfloat16)
-    left = jnp.concatenate(
-        [normed, term_gain, term_bias, jnp.zeros((14, model_width), jnp.bfloat16)], axis=0
-    )
-    right = jnp.concatenate([d_projected, picks], axis=0)
     term = lax.dot_general(
-        left, right, (((0,), (0,)), ((), ())), preferred_element_type=jnp.float32
+        normed, d_projected, (((0,), (0,)), ((), ())), preferred_element_type=jnp.float32
     ).astype(jnp.bfloat16)
-    totals = scatter_sum(apart(term), Z, L)[:shard]
+    lines = -(-shard // 128)
+    ends = 2 * lines + (-(2 * lines + padded // 2)) % 16
+    vectors = jnp.concatenate([term_gain, term_bias], axis=0).astype(jnp.float32)
+    vectors = vectors.reshape(2, L, Z, 2, 2, shard).transpose(4, 1, 3, 2, 0, 5)
+    vectors = jnp.pad(vectors, ((0, 0),) * 5 + ((0, lines * 128 - shard),))
+    vectors = vectors.reshape(2, 2 * L, Z, 2 * lines, 128)
+    vectors = jnp.pad(vectors, ((0, 0),) * 3 + ((0, ends - 2 * lines), (0, 0)))
+    totals = scatter_sum(apart(term), vectors, Z, L)
+    tail = totals[2 * padded : 2 * padded + padded // 2]
+    tail = jnp.concatenate([tail[:, : HD], tail[:, HD:]], axis=0)
+    first = 2 * padded + padded // 2
     return (
         grad_input.astype(jnp.bfloat16),
-        totals[:, :qkv],
-        totals[:, qkv],
-        totals[:, qkv + 1],
+        jnp.concatenate([totals[:shard], totals[padded : padded + shard], tail[:shard]], axis=1),
+        totals[first : first + lines].reshape(-1)[:shard],
+        totals[first + lines : first + 2 * lines].reshape(-1)[:shard],
     )
 
 

time: 230 us -> 215 us (0.935)
  Pallas kernels: 152 us -> 140 us
  other arithmetic: 18 us -> 13.1 us
  matrix products: 35.7 us -> 38.1 us
    pallas_call x1, Pallas kernels: 91.9 us -> 79.8 us  [scatter_sum(): pl.pallas_call(functools.partial(scatter_kernel, Z, L), out_shape=jax.Sha...]
    convert_element_type x1 -> x0, other arithmetic: 4.92 us -> none  [on_device(): normed = (normalized * gain + bias).astype(jnp.bfloat16)]
    dot_general x1, matrix products: 5.32 us -> 7.66 us  [on_device(): jnp.dot(normed, w_all, preferred_element_type=jnp.float32)[:, :qkv]]
    unnamed x18 -> x16, local copies, waits for them, and re-layouts: 9.1 us -> 9.1 us
where the time goes in v3:
time: 215 us
  Pallas kernels  140 us (65%)
  matrix products  38.1 us (18%)
  local copies, waits for them, and re-layouts  14.2 us (7%)
  other arithmetic  13.1 us (6%)
  waiting for transfers between devices  4.58 us (2%)
  between operations  2.43 us (1%)
  starting transfers between devices  2.35 us (1%)
    pallas_call x1, Pallas kernels, scatter_sum(): pl.pallas_call(functools.partial(scatter_kernel, Z, L), out_shape=jax.Sha...  79.8 us
    pallas_call x1, Pallas kernels, gather(): pl.pallas_call(functools.partial(gather_kernel, Z, L), out_shape=(jax.Sha...  60.5 us
    dot_general x1, matrix products, on_device(): lax.dot_general(d_projected, w_all, contract, preferred_element_type=jnp....  13.3 us
    convert_element_type x1, other arithmetic, on_device(): grad_input.astype(jnp.bfloat16)  10.3 us
    unnamed x16, local copies, waits for them, and re-layouts  9.1 us
    dot_general x1, matrix products, on_device(): jnp.dot(normed, w_all, preferred_element_type=jnp.float32)[:, :qkv]  7.66 us
    dot_general x1, matrix products, on_device(): lax.dot_general(picks, w_all, contract, preferred_element_type=jnp.float32)  7.46 us
    dot_general x1, matrix products, on_device(): lax.dot_general(normed, d_projected, (((0,), (0,)), ((), ())), preferred_...  7.18 us
  transfers between devices with their start and end apart: 2, of which 1 were waited for; matrix products, arithmetic and copies ran while one was open for 1% of the time, Pallas kernels for 0%

profile of v3, /device:TPU:0, one launch (start us, length us, event | category | flops | bytes accessed | tf_op | source)
XLA Modules:
  0.0 215.1 jit_solution(10941000498825082955)
XLA Ops:
  0.7 0.8 broadcast_in_dim.26
  1.5 0.8 broadcast_in_dim.27
  2.3 1.2 copy.45
  3.5 0.1 fusion.19.own
  3.7 2.6 %copy-done = bf16[192,14848]{1,0:T(8,128)(2,1)S(1)} copy-done((bf16[192,14848]{1,0:T(8,128)(2,1)S(1)}, bf16[192,14848]{1,0:T(8,128)(2,1)}, u32[]{:S(2)}) %copy-start) | copy-done | bytes 5701656
  6.3 60.5 %shard_map.111 = (bf16[2,4,2,2,464,384]{5,4,3,2,1,0:T(8,128)(2,1)S(1)}, f32[192,128]{1,0:T(8,128)S(1)}, f32[192,128]{1,0:T(8,128)S(1)}) custom-call(bf16[464,384]{1,0:T(8,128)(2,1)S(1)} %fusion.19.own, bf16[192,14848]{1,0:T(8,128)(2,1)S(1)} %copy-done), custom_call_target="tpu_custom_call" | custom-call | tf_op jit(solution)/shard_map/pallas_call | solution.py:214
  66.8 4.2 %copy-done.1 = bf16[2,4,2,2,464,384]{5,4,3,2,1,0:T(8,128)(2,1)} copy-done((bf16[2,4,2,2,464,384]{5,4,3,2,1,0:T(8,128)(2,1)}, bf16[2,4,2,2,464,384]{5,4,3,2,1,0:T(8,128)(2,1)S(1)}, u32[]{:S(2)}) %copy-start.1) | copy-done | bytes 11403288
  71.0 7.5 %fusion.36 = f32[16,14848]{1,0:T(8,128)S(1)} fusion(bf16[14848,384]{1,0:T(8,128)(2,1)} %bitcast.97, s32[16]{0:T(128)S(1)} %iota_add_fusion.1, pred[16]{0:T(512)(128)(4,1)S(1)} %iota_compare_fusion.3), kind=kOutput, calls=%fused_computation.88 | convolution fusion | flops 182464512 | bytes 12353616 | tf_op jit(solution)/shard_map/dot_general | solution.py:438
  78.4 0.3 slice_reduce_fusion.2
  78.7 0.1 slice_reduce_fusion
  78.9 7.7 %fusion.49 = f32[192,384]{1,0:T(8,128)S(1)} fusion(bf16[14848,384]{1,0:T(8,128)(2,1)} %bitcast.98, bf16[192,14848]{1,0:T(8,128)(2,1)S(1)} %bitcast.94, f32[14848]{0:T(1024)S(1)} %get-tuple-element.27, f32[14848]{0:T(1024)S(1)} %get-tuple-element.26, f32[192]{0:T(256)S(1)} %get-tuple-element.50, f32[192]{0:T(256)S(1)} %get-tuple-element.51), kind=kOutput, calls=%fused_computation.110 | convolution fusion | flops 2206531584 | bytes 17520128 | tf_op jit(solution)/shard_map/dot_general | solution.py:444
  86.6 0.1 slice_bitcast_fusion.5
  86.7 0.1 fusion.29
  86.8 0.4 multiply_cosine_fusion
  87.2 0.2 fusion.31
  87.4 0.1 pad_maximum_fusion.4
  87.5 2.2 %collective-permute-start = (bf16[192,128]{1,0:T(8,128)(2,1)S(1)}, bf16[192,128]{1,0:T(8,128)(2,1)S(1)}, u32[]{:S(2)}, u32[]{:S(2)}) collective-permute-start(bf16[192,128]{1,0:T(8,128)(2,1)S(1)} %pad_maximum_fusion.4), channel_id=1, source_target_pairs={{0,1},{1,0},{2,3},{3,2},{4,5},{5,4},{6,7},{7,6},{8,9},{9,8},{10,11... | collective-permute-start | bytes 147464 | tf_op jit(solution)/shard_map/ppermute | solution.py:457
  91.0 1.3 dynamic_slice.3
  92.3 0.7 convert_multiply_fusion
  93.0 0.1 copy.52
  93.1 0.1 copy.48
  93.5 0.1 compare_and_fusion
  93.6 0.1 pad_maximum_fusion.3
  93.7 0.6 fusion.53
  94.3 0.2 fusion.17
  94.5 0.4 fusion.10
  94.9 0.4 convolution_bitcast_fusion.1
  95.3 0.4 fusion.8
  95.7 0.4 convolution_bitcast_fusion.2
  96.1 0.3 convolution_bitcast_fusion.3
  96.4 0.1 pad_maximum_fusion
  96.5 0.2 collective-permute-start.1
  96.8 4.6 %collective-permute-done.1 = f32[192,128]{1,0:T(8,128)S(1)} collective-permute-done((f32[192,128]{1,0:T(8,128)S(1)}, f32[192,128]{1,0:T(8,128)S(1)}, u32[]{:S(2)}, u32[]{:S(2)}) %collective-permute-start.1) | collective-permute-done | bytes 98336 | tf_op jit(solution)/shard_map/ppermute | solution.py:457
  101.3 0.1 fusion.27
  101.5 0.1 copy.59
  101.6 0.1 slice_bitcast_fusion
  101.7 0.2 fusion.33
  101.9 0.1 copy.58
  102.0 13.3 %multiply_reduce_fusion = (bf16[14848]{0:T(1024)(128)(2,1)S(1)}, f32[192]{0:T(256)S(1)}, f32[192]{0:T(256)S(1)}, bf16[14848]{0:T(1024)(128)(2,1)S(1)}, f32[192,14848]{1,0:T(8,128)}) fusion(bf16[192,14848]{1,0:T(8,128)(2,1)} %hidden.1, f32[192]{0:T(256)S(1)} %get-tuple-element.50, f32[192]{0:T(256)S(1)} %get-tuple-element.51, ...), kind=kOutput, calls=%fused_computation.2 | convolution fusion | flops 2218641920 | bytes 28752896 | tf_op jit(solution)/shard_map/dot_general | solution.py:501
  115.3 7.2 %convolution_convert_fusion = bf16[14848,384]{1,0:T(8,128)(2,1)} fusion(bf16[192,64]{0,1:T(8,128)(2,1)S(1)} %copy.59, bf16[192,64]{0,1:T(8,128)(2,1)S(1)} %copy.58, bf16[192,192]{0,1:T(8,128)(2,1)S(1)} %bitcast.105, bf16[192,14848]{1,0:T(8,128)(2,1)S(1)} %bitcast.96, f32[14848]{0:T(1024)S(1)} %get-tuple-element.27, f32[14848]{0:T(1024)S(1)} %get-tuple-element.26, ...), kind=kOutput, calls=%fused_computation.1 | convolution fusion | flops 2212970496 | bytes 17348096 | tf_op jit(solution)/shard_map/dot_general | solution.py:510
  122.5 0.1 convert_element_type.99
  122.6 0.1 convert_element_type.101
  123.0 0.1 reshape.180.vectors
  123.1 79.8 %shard_map.112 = f32[1168,128]{1,0:T(8,128)S(1)} custom-call(bf16[2,4,2,2,464,384]{5,4,3,2,1,0:T(8,128)(2,1)} %bitcast.100, f32[2,4,4,8,128]{4,3,2,1,0:T(8,128)S(1)} %reshape.180.vectors), custom_call_target="tpu_custom_call" | custom-call | tf_op jit(solution)/shard_map/pallas_call | solution.py:388
  202.9 0.6 slice_bitcast_fusion.14
  203.5 0.1 fusion.51
  203.7 1.1 copy.63
  204.8 10.3 %multiply_convert_fusion = bf16[192,14848]{1,0:T(8,128)(2,1)} fusion(bf16[192,14848]{1,0:T(8,128)(2,1)} %hidden.1, f32[192,14848]{1,0:T(8,128)} %get-tuple-element.49, f32[192]{0:T(256)S(1)} %broadcast_multiply_fusion, f32[192]{0:T(256)S(1)} %broadcast_multiply_fusion.1, f32[14848]{0:T(1024)S(1)} %get-tuple-element.26, f32[192]{0:T(256)S(1)} %get-tuple-element.50, ...), kind=kLoop, calls=%fused_computation.3 | loop fusion | flops 25657344 | bytes 22868992 | tf_op jit(solution)/shard_map/convert_element_type | solution.py:525
  (43 shorter events, 0.8 us)
Async XLA Ops:
  3.7 2.6 %copy-start = (bf16[192,14848]{1,0:T(8,128)(2,1)S(1)}, bf16[192,14848]{1,0:T(8,128)(2,1)}, u32[]{:S(2)}) copy-start(bf16[192,14848]{1,0:T(8,128)(2,1)} %hidden.1) | copy-start | bytes 17104900
  6.3 72.6 %slice-start = ((s8[5701632]{0:T(1024)(128)(4,1)}), s8[1507328]{0:T(1024)(128)(4,1)S(1)}, s32[]{:S(2)}) async-start(s8[5701632]{0:T(1024)(128)(4,1)} %bitcast.93), calls=%async_computation | async-start | bytes 3014656
  66.8 4.2 %copy-start.1 = (bf16[2,4,2,2,464,384]{5,4,3,2,1,0:T(8,128)(2,1)}, bf16[2,4,2,2,464,384]{5,4,3,2,1,0:T(8,128)(2,1)S(1)}, u32[]{:S(2)}) copy-start(bf16[2,4,2,2,464,384]{5,4,3,2,1,0:T(8,128)(2,1)S(1)} %get-tuple-element.9) | copy-start | bytes 34209796
  71.0 7.9 %slice-start.1 = ((s8[5701632]{0:T(1024)(128)(4,1)}), s8[4194304]{0:T(1024)(128)(4,1)S(1)}, s32[]{:S(2)}) async-start(s8[5701632]{0:T(1024)(128)(4,1)} %bitcast.93), calls=%async_computation.1 | async-start | bytes 8388608
  78.9 13.4 %copy-start.2 = (bf16[192,192]{1,0:T(8,128)(2,1)S(1)}, bf16[192,192]{1,0:T(8,128)(2,1)}, u32[]{:S(2)}) copy-start(bf16[192,192]{1,0:T(8,128)(2,1)} %param.9) | copy-start | bytes 221188
  87.5 6.1 %collective-permute-start = (bf16[192,128]{1,0:T(8,128)(2,1)S(1)}, bf16[192,128]{1,0:T(8,128)(2,1)S(1)}, u32[]{:S(2)}, u32[]{:S(2)}) collective-permute-start(bf16[192,128]{1,0:T(8,128)(2,1)S(1)} %pad_maximum_fusion.4), channel_id=1, source_target_pairs={{0,1},{1,0},{2,3},{3,2},{4,5},{5,4},{6,7},{7,6},{8,9},{9,8},{10,11... | collective-permute-start | bytes 147464 | tf_op jit(solution)/shard_map/ppermute | solution.py:457
  96.5 4.8 %collective-permute-start.1 = (f32[192,128]{1,0:T(8,128)S(1)}, f32[192,128]{1,0:T(8,128)S(1)}, u32[]{:S(2)}, u32[]{:S(2)}) collective-permute-start(f32[192,128]{1,0:T(8,128)S(1)} %pad_maximum_fusion), channel_id=1, source_target_pairs={{0,1},{1,0},{2,3},{3,2},{4,5},{5,4},{6,7},{7,6},{8,9},{9,8},{10,11... | collective-permute-start | bytes 294920 | tf_op jit(solution)/shard_map/ppermute | solution.py:457
  101.3 14.0 %slice-start.2 = ((s8[5701632]{0:T(1024)(128)(4,1)}), s8[1507328]{0:T(1024)(128)(4,1)S(1)}, s32[]{:S(2)}) async-start(s8[5701632]{0:T(1024)(128)(4,1)} %bitcast.95), calls=%async_computation.2 | async-start | bytes 3014656
  102.0 13.3 %slice-start.3 = ((s8[5701632]{0:T(1024)(128)(4,1)}), s8[4194304]{0:T(1024)(128)(4,1)S(1)}, s32[]{:S(2)}) async-start(s8[5701632]{0:T(1024)(128)(4,1)} %bitcast.95), calls=%async_computation.3 | async-start | bytes 8388608

commit v4 on v3

--- a/solution.py
+++ b/solution.py
@@ -214,7 +214,7 @@
     return pl.pallas_call(
         functools.partial(gather_kernel, Z, L),
         out_shape=(
-            jax.ShapeDtypeStruct((L, Z, 2, 2, rows, LANES), jnp.bfloat16),
+            jax.ShapeDtypeStruct((L, Z, 2, 2, rows, 128), jnp.bfloat16),
             jax.ShapeDtypeStruct((tokens, 128), jnp.float32),
             jax.ShapeDtypeStruct((tokens, 128), jnp.float32),
         ),
@@ -421,27 +421,37 @@
     padded = -(-shard // 16) * 16
     query_cols = QH * HD
 
-    def whole(blocks):
-        return blocks[..., :shard, :].reshape(model_width, LANES)
-
     def apart(rows):
         blocks = rows.reshape(L, Z, 2, 2, shard, LANES)
         return jnp.pad(blocks, ((0, 0),) * 4 + ((0, padded - shard), (0, 0)))
 
-    own_block = jnp.concatenate([w_qkv, ln_gain[:, None], ln_bias[:, None]], axis=1)
-    own_block = jnp.pad(own_block, ((0, padded - shard), (0, LANES - qkv - 2)))
+    lines = -(-shard // HD)
+    fold = -(-(padded + 2 * lines) // 32) * 16
+    pair_rows = jnp.pad(jnp.stack([ln_gain, ln_bias]), ((0, 0), (0, lines * HD - shard)))
+    pair_rows = pair_rows.reshape(2 * lines, HD)
+    w_rows = jnp.pad(w_qkv, ((0, padded - shard), (0, 0)))
+    narrow = jnp.concatenate([w_rows[:, 256:], pair_rows], axis=0)
+    narrow = jnp.pad(narrow, ((0, 2 * fold - narrow.shape[0]), (0, 0)))
+    narrow = jnp.concatenate([narrow[:fold], narrow[fold:]], axis=1)
+    own_block = jnp.concatenate([w_rows[:, :128], w_rows[:, 128:256], narrow], axis=0)
     blocks, centre, variance = gather(own_block, hidden_in, Z, L)
-    w_all = whole(blocks)
-    picks = jnp.arange(16)[:, None] + qkv == jnp.arange(LANES)[None, :]
-    picks = (picks & (jnp.arange(16) < 2)[:, None]).astype(jnp.bfloat16)
+    last = blocks[..., 2 * padded :, :]
+    first_half, second_half = last[..., :HD], last[..., HD:]
+    narrow = jnp.concatenate([first_half, second_half[..., : padded - fold, :]], axis=-2)
+    w_all = jnp.concatenate(
+        [blocks[..., :padded, :], blocks[..., padded : 2 * padded, :], narrow], axis=-1
+    )
+    w_all = w_all[..., :shard, :].reshape(model_width, qkv)
+    ends = second_half[..., padded - fold : padded - fold + 2 * lines, :]
+    ends = ends.reshape(L, Z, 2, 2, 2, lines * HD)[..., :shard].astype(jnp.float32)
+    gain = ends[..., 0, :].reshape(1, model_width)
+    bias = ends[..., 1, :].reshape(1, model_width)
     contract = (((1,), (1,)), ((), ()))
-    rows = lax.dot_general(picks, w_all, contract, preferred_element_type=jnp.float32)
-    gain, bias = rows[0:1], rows[1:2]
     values = hidden_in.astype(jnp.float32)
     inverse = lax.rsqrt(variance[:, :1] + epsilon)
     normalized = (values - centre[:, :1]) * inverse
     normed = (normalized * gain + bias).astype(jnp.bfloat16)
-    proj_total = jnp.dot(normed, w_all, preferred_element_type=jnp.float32)[:, :qkv]
+    proj_total = jnp.dot(normed, w_all, preferred_element_type=jnp.float32)
     positions = lax.axis_index("local") * tok_rows + jnp.arange(tok_rows, dtype=jnp.int32)
     cosine, sine_table = rope_tables(positions, HD)
     query = rotate(proj_total[:, :query_cols].reshape(tok_rows, QH, HD), cosine, sine_table).astype(
@@ -497,7 +507,7 @@
     d_query_pre = unrotate(d_query, cosine, sine_table).reshape(tok_rows, query_cols)
     d_key_pre = unrotate(d_pair[:, None, :HD], cosine, sine_table)[:, 0, :]
     d_projected = jnp.concatenate([d_query_pre, d_key_pre, d_pair[:, HD:]], axis=1)
-    d_projected = jnp.pad(d_projected.astype(jnp.bfloat16), ((0, 0), (0, LANES - qkv)))
+    d_projected = d_projected.astype(jnp.bfloat16)
     d_normed = lax.dot_general(d_projected, w_all, contract, preferred_element_type=jnp.float32)
     grad_hat = d_normed * gain
     grad_input = inverse * (
@@ -507,8 +517,9 @@
     )
     term_gain = jnp.sum(d_normed * normalized, axis=0, keepdims=True).astype(jnp.bfloat16)
     term_bias = jnp.sum(d_normed, axis=0, keepdims=True).astype(jnp.bfloat16)
+    d_padded = jnp.pad(d_projected, ((0, 0), (0, LANES - qkv)))
     term = lax.dot_general(
-        normed, d_projected, (((0,), (0,)), ((), ())), preferred_element_type=jnp.float32
+        normed, d_padded, (((0,), (0,)), ((), ())), preferred_element_type=jnp.float32
     ).astype(jnp.bfloat16)
     lines = -(-shard // 128)
     ends = 2 * lines + (-(2 * lines + padded // 2)) % 16

time: 215 us -> 210 us (0.977)
  matrix products: 38.1 us -> 26 us
  Pallas kernels: 140 us -> 131 us
  other arithmetic: 13.1 us -> 21.8 us
  local copies, waits for them, and re-layouts: 14.2 us -> 22.1 us
    dot_general x3 -> x2, matrix products: 22.3 us -> 10.6 us  [the longest x1 7.17 us: on_device(): lax.dot_general(normed, d_padded, (((0,), (0,)), ((), ())), preferred_ele...]
    slice x1 -> x8, local copies, waits for them, and re-layouts: 0.31 us -> 9.13 us  [the longest x1 3.38 us: on_device(): blocks[..., :padded, :]]
    concatenate x1 -> x3, other arithmetic: 0.14 us -> 8.74 us  [the longest x1 8.62 us: on_device(): jnp.concatenate([blocks[..., :padded, :], blocks[..., padded:2 * padded,...]
    pallas_call x1, Pallas kernels: 60.5 us -> 53 us  [gather(): pl.pallas_call(functools.partial(gather_kernel, Z, L), out_shape=(jax.Sha...]
    unnamed x16 -> x27, local copies, waits for them, and re-layouts: 9.1 us -> 4.99 us
where the time goes in v4:
time: 210 us
  Pallas kernels  131 us (62%)
  matrix products  26 us (12%)
  local copies, waits for them, and re-layouts  22.1 us (11%)
  other arithmetic  21.8 us (10%)
  waiting for transfers between devices  3.91 us (2%)
  between operations  2.52 us (1%)
  starting transfers between devices  2.16 us (1%)
    pallas_call x1, Pallas kernels, scatter_sum(): pl.pallas_call(functools.partial(scatter_kernel, Z, L), out_shape=jax.Sha...  78.2 us
    pallas_call x1, Pallas kernels, gather(): pl.pallas_call(functools.partial(gather_kernel, Z, L), out_shape=(jax.Sha...  53 us
    dot_general x1, matrix products, on_device(): lax.dot_general(d_projected, w_all, contract, preferred_element_type=jnp....  12.9 us
    convert_element_type x1, other arithmetic, on_device(): grad_input.astype(jnp.bfloat16)  10.3 us
    concatenate x1, other arithmetic, on_device(): jnp.concatenate([blocks[..., :padded, :], blocks[..., padded:2 * padded,...  8.62 us
    dot_general x1, matrix products, on_device(): lax.dot_general(normed, d_padded, (((0,), (0,)), ((), ())), preferred_ele...  7.17 us
    unnamed x27, local copies, waits for them, and re-layouts  4.99 us
  transfers between devices with their start and end apart: 2, of which 1 were waited for; matrix products, arithmetic and copies ran while one was open for 1% of the time, Pallas kernels for 0%

profile of v4, /device:TPU:0, one launch (start us, length us, event | category | flops | bytes accessed | tf_op | source)
XLA Modules:
  0.0 209.6 jit_solution(4598679270583533791)
XLA Ops:
  0.6 0.8 slice.136
  1.5 0.8 slice.135
  2.2 1.0 fusion.47
  3.2 0.7 stack.10
  3.9 0.7 stack.9
  4.7 0.1 copy.84
  4.8 0.1 copy.83
  5.0 0.2 copy.82
  5.1 0.2 copy.81
  5.4 2.6 %copy-done = bf16[192,14848]{1,0:T(8,128)(2,1)S(1)} copy-done((bf16[192,14848]{1,0:T(8,128)(2,1)S(1)}, bf16[192,14848]{1,0:T(8,128)(2,1)}, u32[]{:S(2)}) %copy-start) | copy-done | bytes 5701656
  8.0 53.0 %shard_map.111 = (bf16[2,4,2,2,1168,128]{5,4,3,2,1,0:T(8,128)(2,1)S(1)}, f32[192,128]{1,0:T(8,128)S(1)}, f32[192,128]{1,0:T(8,128)S(1)}) custom-call(bf16[1168,128]{1,0:T(8,128)(2,1)S(1)} %fusion.17.own, bf16[192,14848]{1,0:T(8,128)(2,1)S(1)} %copy-done), custom_call_target="tpu_custom_call" | custom-call | tf_op jit(solution)/shard_map/pallas_call | solution.py:214
  61.1 0.6 slice.147
  61.7 1.4 slice.146
  63.1 3.4 %fusion.44 = (bf16[2,4,2,2,464,128]{5,4,3,2,1,0:T(8,128)(2,1)}, bf16[2,4,2,2,464,128]{5,4,3,2,1,0:T(8,128)(2,1)}) fusion(bf16[2,4,2,2,1168,128]{5,4,3,2,1,0:T(8,128)(2,1)S(1)} %get-tuple-element.9), kind=kLoop, calls=%fused_computation.109 | loop fusion | bytes 15204352 | tf_op jit(solution)/shard_map/slice | solution.py:442
  66.5 0.1 reshape.171
  66.7 1.0 slice_reduce_fusion.2
  67.7 1.6 mul.155
  69.3 1.6 add.87
  70.9 0.1 slice_reduce_fusion
  71.1 8.6 %maximum_maximum_fusion = bf16[2,4,2,2,464,320]{5,4,3,2,1,0:T(8,128)(2,1)S(1)} fusion(bf16[2,4,2,2,224,64]{5,4,3,2,1,0:T(8,128)(2,1)S(1)} %slice.147, bf16[2,4,2,2,240,64]{5,4,3,2,1,0:T(8,128)(2,1)} %slice.146, bf16[2,4,2,2,464,128]{5,4,3,2,1,0:T(8,128)(2,1)} %get-tuple-element.29, bf16[2,4,2,2,464,128]{5,4,3,2,1,0:T(8,128)(2,1)} %get-tuple-element.28), kind=kLoop, calls=%fused_computation.2 | loop fusion | flops 38010880 | bytes 19005440 | tf_op jit(solution)/shard_map/concatenate | solution.py:441
  79.8 3.4 %fusion.43 = f32[192,320]{1,0:T(8,128)S(1)} fusion(bf16[14848,320]{1,0:T(8,128)(2,1)S(1)} %bitcast.98, bf16[192,14848]{1,0:T(8,128)(2,1)S(1)} %bitcast.95, f32[14848]{0:T(1024)S(1)} %copy-done.5, f32[14848]{0:T(1024)S(1)} %copy-done.2, f32[192]{0:T(256)S(1)} %get-tuple-element.54, f32[192]{0:T(256)S(1)} %get-tuple-element.55), kind=kOutput, calls=%fused_computation.108 | convolution fusion | flops 1841627136 | bytes 15570432 | tf_op jit(solution)/shard_map/dot_general | solution.py:454
  83.2 0.7 copy-done.1
  84.1 0.4 multiply_cosine_fusion
  84.5 0.2 fusion.28
  84.8 1.3 collective-permute-start
  86.2 0.1 copy.53
  87.8 1.3 dynamic_slice.3
  89.1 0.7 convert_multiply_fusion
  89.7 0.1 copy.57
  89.9 0.1 compare_and_fusion
  90.2 0.6 fusion.49
  90.8 0.2 fusion.14
  90.9 0.4 convolution_bitcast_fusion.1
  91.3 0.4 fusion.10
  91.7 0.4 fusion.8
  92.2 0.4 convolution_bitcast_fusion.2
  92.5 0.3 convolution_bitcast_fusion.3
  92.9 0.9 collective-permute-start.1
  93.9 3.9 %collective-permute-done.1 = f32[192,128]{1,0:T(8,128)S(1)} collective-permute-done((f32[192,128]{1,0:T(8,128)S(1)}, f32[192,128]{1,0:T(8,128)S(1)}, u32[]{:S(2)}, u32[]{:S(2)}) %collective-permute-start.1) | collective-permute-done | bytes 98336 | tf_op jit(solution)/shard_map/ppermute | solution.py:467
  98.2 0.2 fusion.30
  98.5 12.9 %multiply_reduce_fusion = (bf16[14848]{0:T(1024)(128)(2,1)S(1)}, f32[192]{0:T(256)S(1)}, f32[192]{0:T(256)S(1)}, bf16[14848]{0:T(1024)(128)(2,1)S(1)}, f32[192,14848]{1,0:T(8,128)}) fusion(bf16[192,14848]{1,0:T(8,128)(2,1)} %hidden.1, f32[192]{0:T(256)S(1)} %get-tuple-element.54, f32[192]{0:T(256)S(1)} %get-tuple-element.55, f32[14848]{0:T(1024)S(1)} %copy-done.3, ...), kind=kOutput, calls=%fused_computation.3 | convolution fusion | flops 1853368832 | bytes 26852352 | tf_op jit(solution)/shard_map/dot_general | solution.py:511
  111.5 7.2 %convolution_convert_fusion = bf16[14848,384]{1,0:T(8,128)(2,1)} fusion(bf16[192,320]{0,1:T(8,128)(2,1)S(1)} %pad_maximum_fusion, bf16[192,14848]{1,0:T(8,128)(2,1)S(1)} %bitcast.97, f32[14848]{0:T(1024)S(1)} %copy-done.6, f32[14848]{0:T(1024)S(1)} %copy-done.3, f32[192]{0:T(256)S(1)} %get-tuple-element.54, f32[192]{0:T(256)S(1)} %get-tuple-element.55), kind=kOutput, calls=%fused_computation.1 | convolution fusion | flops 2212233216 | bytes 17348096 | tf_op jit(solution)/shard_map/dot_general | solution.py:521
  118.7 0.1 convert_element_type.104
  118.8 0.1 convert_element_type.102
  119.2 78.2 %shard_map.112 = f32[1168,128]{1,0:T(8,128)S(1)} custom-call(bf16[2,4,2,2,464,384]{5,4,3,2,1,0:T(8,128)(2,1)} %bitcast.100, f32[2,4,4,8,128]{4,3,2,1,0:T(8,128)S(1)} %reshape.181.vectors), custom_call_target="tpu_custom_call" | custom-call | tf_op jit(solution)/shard_map/pallas_call | solution.py:388
  197.6 0.6 slice_bitcast_fusion.14
  198.3 1.1 copy.68
  199.4 10.3 %multiply_convert_fusion = bf16[192,14848]{1,0:T(8,128)(2,1)} fusion(bf16[192,14848]{1,0:T(8,128)(2,1)} %hidden.1, f32[192,14848]{1,0:T(8,128)} %get-tuple-element.53, f32[192]{0:T(256)S(1)} %broadcast_multiply_fusion, f32[192]{0:T(256)S(1)} %broadcast_multiply_fusion.1, f32[14848]{0:T(1024)S(1)} %copy-done.3, f32[192]{0:T(256)S(1)} %get-tuple-element.54, ...), kind=kLoop, calls=%fused_computation.4 | loop fusion | flops 25657344 | bytes 22868992 | tf_op jit(solution)/shard_map/convert_element_type | solution.py:536
  (66 shorter events, 2.2 us)
Async XLA Ops:
  5.4 2.6 %copy-start = (bf16[192,14848]{1,0:T(8,128)(2,1)S(1)}, bf16[192,14848]{1,0:T(8,128)(2,1)}, u32[]{:S(2)}) copy-start(bf16[192,14848]{1,0:T(8,128)(2,1)} %hidden.1) | copy-start | bytes 17104900
  66.7 13.0 %slice-start = ((s8[5701632]{0:T(1024)(128)(4,1)}), s8[1507328]{0:T(1024)(128)(4,1)S(1)}, s32[]{:S(2)}) async-start(s8[5701632]{0:T(1024)(128)(4,1)} %bitcast.94), calls=%async_computation | async-start | bytes 3014656
  71.1 8.7 %slice-start.1 = ((s8[5701632]{0:T(1024)(128)(4,1)}), s8[4194304]{0:T(1024)(128)(4,1)S(1)}, s32[]{:S(2)}) async-start(s8[5701632]{0:T(1024)(128)(4,1)} %bitcast.94), calls=%async_computation.1 | async-start | bytes 8388608
  71.1 8.7 %copy-start.2 = (f32[14848]{0:T(1024)S(1)}, f32[14848]{0:T(1024)}, u32[]{:S(2)}) copy-start(f32[14848]{0:T(1024)} %mul.155) | copy-start | bytes 178180
  71.1 8.7 %copy-start.5 = (f32[14848]{0:T(1024)S(1)}, f32[14848]{0:T(1024)}, u32[]{:S(2)}) copy-start(f32[14848]{0:T(1024)} %add.87) | copy-start | bytes 178180
  79.7 4.2 %copy-start.1 = (bf16[2,4,2,2,464,320]{5,4,3,2,1,0:T(8,128)(2,1)}, bf16[2,4,2,2,464,320]{5,4,3,2,1,0:T(8,128)(2,1)S(1)}, u32[]{:S(2)}) copy-start(bf16[2,4,2,2,464,320]{5,4,3,2,1,0:T(8,128)(2,1)S(1)} %maximum_maximum_fusion) | copy-start | bytes 28508164
  79.8 9.3 %copy-start.4 = (bf16[192,192]{1,0:T(8,128)(2,1)S(1)}, bf16[192,192]{1,0:T(8,128)(2,1)}, u32[]{:S(2)}) copy-start(bf16[192,192]{1,0:T(8,128)(2,1)} %param.9) | copy-start | bytes 221188
  83.9 14.5 %copy-start.3 = (f32[14848]{0:T(1024)S(1)}, f32[14848]{0:T(1024)}, u32[]{:S(2)}) copy-start(f32[14848]{0:T(1024)} %mul.155) | copy-start | bytes 178180
  84.8 5.3 %collective-permute-start = (bf16[192,128]{1,0:T(8,128)(2,1)S(1)}, bf16[192,128]{1,0:T(8,128)(2,1)S(1)}, u32[]{:S(2)}, u32[]{:S(2)}) collective-permute-start(bf16[192,128]{1,0:T(8,128)(2,1)S(1)} %pad_maximum_fusion.5), channel_id=1, source_target_pairs={{0,1},{1,0},{2,3},{3,2},{4,5},{5,4},{6,7},{7,6},{8,9},{9,8},{10,11... | collective-permute-start | bytes 147464 | tf_op jit(solution)/shard_map/ppermute | solution.py:467
  92.9 4.8 %collective-permute-start.1 = (f32[192,128]{1,0:T(8,128)S(1)}, f32[192,128]{1,0:T(8,128)S(1)}, u32[]{:S(2)}, u32[]{:S(2)}) collective-permute-start(f32[192,128]{1,0:T(8,128)S(1)} %pad_maximum_fusion.1), channel_id=1, source_target_pairs={{0,1},{1,0},{2,3},{3,2},{4,5},{5,4},{6,7},{7,6},{8,9},{9,8},{10,11... | collective-permute-start | bytes 294920 | tf_op jit(solution)/shard_map/ppermute | solution.py:467
  93.8 17.6 %slice-start.2 = ((s8[5701632]{0:T(1024)(128)(4,1)}), s8[1507328]{0:T(1024)(128)(4,1)S(1)}, s32[]{:S(2)}) async-start(s8[5701632]{0:T(1024)(128)(4,1)} %bitcast.96), calls=%async_computation.2 | async-start | bytes 3014656
  98.4 13.0 %slice-start.3 = ((s8[5701632]{0:T(1024)(128)(4,1)}), s8[4194304]{0:T(1024)(128)(4,1)S(1)}, s32[]{:S(2)}) async-start(s8[5701632]{0:T(1024)(128)(4,1)} %bitcast.96), calls=%async_computation.3 | async-start | bytes 8388608
  98.4 13.0 %copy-start.6 = (f32[14848]{0:T(1024)S(1)}, f32[14848]{0:T(1024)}, u32[]{:S(2)}) copy-start(f32[14848]{0:T(1024)} %add.87) | copy-start | bytes 178180

commit v5 on v4

--- a/solution.py
+++ b/solution.py
@@ -144,7 +144,10 @@
         variance[span, :] = jnp.broadcast_to(spread_of, (16, 128))
         return carry
 
-    lax.fori_loop(0, held.shape[0] // 16, stats, 0)
+    groups = held.shape[0] // 16
+
+    def some_stats(k):
+        lax.fori_loop(k * groups // Z, (k + 1) * groups // Z, stats, 0)
 
     def spread(k):
         zz = (z + Z - k) % Z
@@ -168,10 +171,12 @@
     def middle(k, carry):
         spread(k)
         relay(k - 1)
+        some_stats(k - 1)
         return carry
 
     lax.fori_loop(1, Z, middle, 0)
     relay(Z - 1)
+    some_stats(Z - 1)
 
     def corners(k, carry):
         zz = (z + Z - k) % Z

time: 210 us -> 210 us (level)
  no operation moved by 1% of the time
where the time goes in v5:
time: 210 us
  Pallas kernels  131 us (62%)
  matrix products  26 us (12%)
  local copies, waits for them, and re-layouts  22.1 us (11%)
  other arithmetic  21.8 us (10%)
  waiting for transfers between devices  3.91 us (2%)
  between operations  2.52 us (1%)
  starting transfers between devices  2.16 us (1%)
    pallas_call x1, Pallas kernels, scatter_sum(): pl.pallas_call(functools.partial(scatter_kernel, Z, L), out_shape=jax.Sha...  78.2 us
    pallas_call x1, Pallas kernels, gather(): pl.pallas_call(functools.partial(gather_kernel, Z, L), out_shape=(jax.Sha...  53 us
    dot_general x1, matrix products, on_device(): lax.dot_general(d_projected, w_all, contract, preferred_element_type=jnp....  12.9 us
    convert_element_type x1, other arithmetic, on_device(): grad_input.astype(jnp.bfloat16)  10.3 us
    concatenate x1, other arithmetic, on_device(): jnp.concatenate([blocks[..., :padded, :], blocks[..., padded:2 * padded,...  8.62 us
    dot_general x1, matrix products, on_device(): lax.dot_general(normed, d_padded, (((0,), (0,)), ((), ())), preferred_ele...  7.17 us
    unnamed x27, local copies, waits for them, and re-layouts  4.99 us
  transfers between devices with their start and end apart: 2, of which 1 were waited for; matrix products, arithmetic and copies ran while one was open for 1% of the time, Pallas kernels for 0%

profile of v5, /device:TPU:0, one launch (start us, length us, event | category | flops | bytes accessed | tf_op | source)
XLA Modules:
  0.0 209.6 jit_solution(5898176246163185866)
XLA Ops:
  0.6 0.8 slice.136
  1.5 0.8 slice.135
  2.2 1.0 fusion.47
  3.2 0.7 stack.10
  3.9 0.7 stack.9
  4.7 0.1 copy.84
  4.8 0.1 copy.83
  5.0 0.2 copy.82
  5.1 0.2 copy.81
  5.4 2.6 %copy-done = bf16[192,14848]{1,0:T(8,128)(2,1)S(1)} copy-done((bf16[192,14848]{1,0:T(8,128)(2,1)S(1)}, bf16[192,14848]{1,0:T(8,128)(2,1)}, u32[]{:S(2)}) %copy-start) | copy-done | bytes 5701656
  8.0 53.0 %shard_map.111 = (bf16[2,4,2,2,1168,128]{5,4,3,2,1,0:T(8,128)(2,1)S(1)}, f32[192,128]{1,0:T(8,128)S(1)}, f32[192,128]{1,0:T(8,128)S(1)}) custom-call(bf16[1168,128]{1,0:T(8,128)(2,1)S(1)} %fusion.17.own, bf16[192,14848]{1,0:T(8,128)(2,1)S(1)} %copy-done), custom_call_target="tpu_custom_call" | custom-call | tf_op jit(solution)/shard_map/pallas_call | solution.py:219
  61.1 0.6 slice.147
  61.7 1.4 slice.146
  63.1 3.4 %fusion.44 = (bf16[2,4,2,2,464,128]{5,4,3,2,1,0:T(8,128)(2,1)}, bf16[2,4,2,2,464,128]{5,4,3,2,1,0:T(8,128)(2,1)}) fusion(bf16[2,4,2,2,1168,128]{5,4,3,2,1,0:T(8,128)(2,1)S(1)} %get-tuple-element.9), kind=kLoop, calls=%fused_computation.109 | loop fusion | bytes 15204352 | tf_op jit(solution)/shard_map/slice | solution.py:447
  66.5 0.1 reshape.171
  66.7 1.0 slice_reduce_fusion.2
  67.7 1.6 mul.155
  69.3 1.6 add.87
  70.9 0.1 slice_reduce_fusion
  71.1 8.6 %maximum_maximum_fusion = bf16[2,4,2,2,464,320]{5,4,3,2,1,0:T(8,128)(2,1)S(1)} fusion(bf16[2,4,2,2,224,64]{5,4,3,2,1,0:T(8,128)(2,1)S(1)} %slice.147, bf16[2,4,2,2,240,64]{5,4,3,2,1,0:T(8,128)(2,1)} %slice.146, bf16[2,4,2,2,464,128]{5,4,3,2,1,0:T(8,128)(2,1)} %get-tuple-element.29, bf16[2,4,2,2,464,128]{5,4,3,2,1,0:T(8,128)(2,1)} %get-tuple-element.28), kind=kLoop, calls=%fused_computation.2 | loop fusion | flops 38010880 | bytes 19005440 | tf_op jit(solution)/shard_map/concatenate | solution.py:446
  79.8 3.4 %fusion.43 = f32[192,320]{1,0:T(8,128)S(1)} fusion(bf16[14848,320]{1,0:T(8,128)(2,1)S(1)} %bitcast.98, bf16[192,14848]{1,0:T(8,128)(2,1)S(1)} %bitcast.95, f32[14848]{0:T(1024)S(1)} %copy-done.5, f32[14848]{0:T(1024)S(1)} %copy-done.2, f32[192]{0:T(256)S(1)} %get-tuple-element.54, f32[192]{0:T(256)S(1)} %get-tuple-element.55), kind=kOutput, calls=%fused_computation.108 | convolution fusion | flops 1841627136 | bytes 15570432 | tf_op jit(solution)/shard_map/dot_general | solution.py:459
  83.2 0.7 copy-done.1
  84.1 0.4 multiply_cosine_fusion
  84.5 0.2 fusion.28
  84.8 1.3 collective-permute-start
  86.2 0.1 copy.53
  87.8 1.3 dynamic_slice.3
  89.1 0.7 convert_multiply_fusion
  89.7 0.1 copy.57
  89.9 0.1 compare_and_fusion
  90.2 0.6 fusion.49
  90.8 0.2 fusion.14
  90.9 0.4 convolution_bitcast_fusion.1
  91.3 0.4 fusion.10
  91.7 0.4 fusion.8
  92.2 0.4 convolution_bitcast_fusion.2
  92.5 0.3 convolution_bitcast_fusion.3
  92.9 0.9 collective-permute-start.1
  93.9 3.9 %collective-permute-done.1 = f32[192,128]{1,0:T(8,128)S(1)} collective-permute-done((f32[192,128]{1,0:T(8,128)S(1)}, f32[192,128]{1,0:T(8,128)S(1)}, u32[]{:S(2)}, u32[]{:S(2)}) %collective-permute-start.1) | collective-permute-done | bytes 98336 | tf_op jit(solution)/shard_map/ppermute | solution.py:472
  98.2 0.2 fusion.30
  98.5 12.9 %multiply_reduce_fusion = (bf16[14848]{0:T(1024)(128)(2,1)S(1)}, f32[192]{0:T(256)S(1)}, f32[192]{0:T(256)S(1)}, bf16[14848]{0:T(1024)(128)(2,1)S(1)}, f32[192,14848]{1,0:T(8,128)}) fusion(bf16[192,14848]{1,0:T(8,128)(2,1)} %hidden.1, f32[192]{0:T(256)S(1)} %get-tuple-element.54, f32[192]{0:T(256)S(1)} %get-tuple-element.55, f32[14848]{0:T(1024)S(1)} %copy-done.3, ...), kind=kOutput, calls=%fused_computation.3 | convolution fusion | flops 1853368832 | bytes 26852352 | tf_op jit(solution)/shard_map/dot_general | solution.py:516
  111.5 7.2 %convolution_convert_fusion = bf16[14848,384]{1,0:T(8,128)(2,1)} fusion(bf16[192,320]{0,1:T(8,128)(2,1)S(1)} %pad_maximum_fusion, bf16[192,14848]{1,0:T(8,128)(2,1)S(1)} %bitcast.97, f32[14848]{0:T(1024)S(1)} %copy-done.6, f32[14848]{0:T(1024)S(1)} %copy-done.3, f32[192]{0:T(256)S(1)} %get-tuple-element.54, f32[192]{0:T(256)S(1)} %get-tuple-element.55), kind=kOutput, calls=%fused_computation.1 | convolution fusion | flops 2212233216 | bytes 17348096 | tf_op jit(solution)/shard_map/dot_general | solution.py:526
  118.7 0.1 convert_element_type.104
  118.8 0.1 convert_element_type.102
  119.2 78.2 %shard_map.112 = f32[1168,128]{1,0:T(8,128)S(1)} custom-call(bf16[2,4,2,2,464,384]{5,4,3,2,1,0:T(8,128)(2,1)} %bitcast.100, f32[2,4,4,8,128]{4,3,2,1,0:T(8,128)S(1)} %reshape.181.vectors), custom_call_target="tpu_custom_call" | custom-call | tf_op jit(solution)/shard_map/pallas_call | solution.py:393
  197.6 0.6 slice_bitcast_fusion.14
  198.3 1.1 copy.68
  199.4 10.3 %multiply_convert_fusion = bf16[192,14848]{1,0:T(8,128)(2,1)} fusion(bf16[192,14848]{1,0:T(8,128)(2,1)} %hidden.1, f32[192,14848]{1,0:T(8,128)} %get-tuple-element.53, f32[192]{0:T(256)S(1)} %broadcast_multiply_fusion, f32[192]{0:T(256)S(1)} %broadcast_multiply_fusion.1, f32[14848]{0:T(1024)S(1)} %copy-done.3, f32[192]{0:T(256)S(1)} %get-tuple-element.54, ...), kind=kLoop, calls=%fused_computation.4 | loop fusion | flops 25657344 | bytes 22868992 | tf_op jit(solution)/shard_map/convert_element_type | solution.py:541
  (66 shorter events, 2.2 us)
Async XLA Ops:
  5.4 2.6 %copy-start = (bf16[192,14848]{1,0:T(8,128)(2,1)S(1)}, bf16[192,14848]{1,0:T(8,128)(2,1)}, u32[]{:S(2)}) copy-start(bf16[192,14848]{1,0:T(8,128)(2,1)} %hidden.1) | copy-start | bytes 17104900
  66.7 13.0 %slice-start = ((s8[5701632]{0:T(1024)(128)(4,1)}), s8[1507328]{0:T(1024)(128)(4,1)S(1)}, s32[]{:S(2)}) async-start(s8[5701632]{0:T(1024)(128)(4,1)} %bitcast.94), calls=%async_computation | async-start | bytes 3014656
  71.1 8.7 %slice-start.1 = ((s8[5701632]{0:T(1024)(128)(4,1)}), s8[4194304]{0:T(1024)(128)(4,1)S(1)}, s32[]{:S(2)}) async-start(s8[5701632]{0:T(1024)(128)(4,1)} %bitcast.94), calls=%async_computation.1 | async-start | bytes 8388608
  71.1 8.7 %copy-start.2 = (f32[14848]{0:T(1024)S(1)}, f32[14848]{0:T(1024)}, u32[]{:S(2)}) copy-start(f32[14848]{0:T(1024)} %mul.155) | copy-start | bytes 178180
  71.1 8.7 %copy-start.5 = (f32[14848]{0:T(1024)S(1)}, f32[14848]{0:T(1024)}, u32[]{:S(2)}) copy-start(f32[14848]{0:T(1024)} %add.87) | copy-start | bytes 178180
  79.7 4.2 %copy-start.1 = (bf16[2,4,2,2,464,320]{5,4,3,2,1,0:T(8,128)(2,1)}, bf16[2,4,2,2,464,320]{5,4,3,2,1,0:T(8,128)(2,1)S(1)}, u32[]{:S(2)}) copy-start(bf16[2,4,2,2,464,320]{5,4,3,2,1,0:T(8,128)(2,1)S(1)} %maximum_maximum_fusion) | copy-start | bytes 28508164
  79.8 9.3 %copy-start.4 = (bf16[192,192]{1,0:T(8,128)(2,1)S(1)}, bf16[192,192]{1,0:T(8,128)(2,1)}, u32[]{:S(2)}) copy-start(bf16[192,192]{1,0:T(8,128)(2,1)} %param.9) | copy-start | bytes 221188
  83.9 14.5 %copy-start.3 = (f32[14848]{0:T(1024)S(1)}, f32[14848]{0:T(1024)}, u32[]{:S(2)}) copy-start(f32[14848]{0:T(1024)} %mul.155) | copy-start | bytes 178180
  84.8 5.3 %collective-permute-start = (bf16[192,128]{1,0:T(8,128)(2,1)S(1)}, bf16[192,128]{1,0:T(8,128)(2,1)S(1)}, u32[]{:S(2)}, u32[]{:S(2)}) collective-permute-start(bf16[192,128]{1,0:T(8,128)(2,1)S(1)} %pad_maximum_fusion.5), channel_id=1, source_target_pairs={{0,1},{1,0},{2,3},{3,2},{4,5},{5,4},{6,7},{7,6},{8,9},{9,8},{10,11... | collective-permute-start | bytes 147464 | tf_op jit(solution)/shard_map/ppermute | solution.py:472
  92.9 4.8 %collective-permute-start.1 = (f32[192,128]{1,0:T(8,128)S(1)}, f32[192,128]{1,0:T(8,128)S(1)}, u32[]{:S(2)}, u32[]{:S(2)}) collective-permute-start(f32[192,128]{1,0:T(8,128)S(1)} %pad_maximum_fusion.1), channel_id=1, source_target_pairs={{0,1},{1,0},{2,3},{3,2},{4,5},{5,4},{6,7},{7,6},{8,9},{9,8},{10,11... | collective-permute-start | bytes 294920 | tf_op jit(solution)/shard_map/ppermute | solution.py:472
  93.8 17.6 %slice-start.2 = ((s8[5701632]{0:T(1024)(128)(4,1)}), s8[1507328]{0:T(1024)(128)(4,1)S(1)}, s32[]{:S(2)}) async-start(s8[5701632]{0:T(1024)(128)(4,1)} %bitcast.96), calls=%async_computation.2 | async-start | bytes 3014656
  98.4 13.0 %slice-start.3 = ((s8[5701632]{0:T(1024)(128)(4,1)}), s8[4194304]{0:T(1024)(128)(4,1)S(1)}, s32[]{:S(2)}) async-start(s8[5701632]{0:T(1024)(128)(4,1)} %bitcast.96), calls=%async_computation.3 | async-start | bytes 8388608
  98.4 13.0 %copy-start.6 = (f32[14848]{0:T(1024)S(1)}, f32[14848]{0:T(1024)}, u32[]{:S(2)}) copy-start(f32[14848]{0:T(1024)} %add.87) | copy-start | bytes 178180
